TPU v7x, 256 devices: a whole 4x4x8 slice. The times are simulated.
256 devices in a mesh: member: 8 (over y, z_hi), space: 32 (over z_lo, x, core).
Axes of the slice: x: 4, y: 4, z: 8 (z_hi: 2, z_lo: 4; z = z_hi * 4 + z_lo), core: 2. Of those that a mesh axis runs over, the one named last changes fastest.
Arguments:
- hidden_state: bfloat16 [8, 128, 512, 1024], P('member', 'space'), may hold values from -6 to 6
- proj_weight: bfloat16 [100, 1024], replicated, may hold values from -0.1875 to 0.1875
- output_offset_vector: float32 [100], replicated, may hold values from -3 to 3
- verifying_reanalysis: float32 [100, 128, 512], P(None, 'space'), may hold values from -6 to 6
- counts: int32 [128], P('space'), may hold values from 128 to 512, as said below
- var_weight: float32 [100], replicated, may hold values from 0.25 to 4
Outputs:
- latent_grad: bfloat16 [8, 128, 512, 1024], P('member', 'space')
- weight_grad: float32 [100, 1024], replicated
- bias_grad: float32 [100], replicated
- loss: float32 [], replicated
Inputs may be any that keep to these rules, and one draw needn't show every extreme that they name: `counts`: row 0 has all 512 slots live; lengths decrease on average with the row index, with random variation from row to row.
All inputs are finite; a program needn't handle non-finite values.
Results may differ from a plain program's by a relative error of at most 0.0049.
Values sent between devices are 32-bit elements; how exact they have to be, the bound alone decides.
A program may use at most 64 MiB of HBM per device.

v0:
```python
import math

import jax
import jax.numpy as jnp
from jax import lax
from jax.sharding import PartitionSpec as P

SMOOTHING = 0.05
FAIRNESS = 0.95
GRAD_SCALE = 16.0
LATITUDE_SPAN = 80.0


def smooth_abs(values):
    return jnp.sqrt(values * values + SMOOTHING * SMOOTHING) - SMOOTHING


def smooth_sign(values):
    return values / jnp.sqrt(values * values + SMOOTHING * SMOOTHING)


def finish_field(
    fields,
    truth_part,
    weight_part_pts,
    variable_scale,
    polarity_totals,
    modulus_totals,
    ensemble_members,
):
    coeff = FAIRNESS / (ensemble_members * (ensemble_members - 1)) + (1.0 - FAIRNESS) / (
        ensemble_members * ensemble_members
    )
    observation_misfit = fields - truth_part
    total = jnp.sum(
        weight_part_pts
        * variable_scale
        * (smooth_abs(observation_misfit) / ensemble_members - 0.5 * coeff * modulus_totals)
    )
    field = (
        weight_part_pts
        * variable_scale
        * (smooth_sign(observation_misfit) / ensemble_members - coeff * polarity_totals)
    )
    return (field, total)


def per_device(
    hidden_state, proj_weight, output_offset_vector, verifying_reanalysis, counts, var_weight
):
    quantity_tally, stored_latitude_lines, realization_indices = verifying_reanalysis.shape
    width = proj_weight.shape[1]
    ensemble_members = lax.axis_size("member")
    total_rows = stored_latitude_lines * lax.axis_size("space")
    points = stored_latitude_lines * realization_indices
    row_index = (
        lax.axis_index("space") * stored_latitude_lines
        + jnp.arange(stored_latitude_lines, dtype=jnp.int32)
    ).astype(jnp.float32)
    latitude = (row_index + 0.5) * (LATITUDE_SPAN / total_rows) * (math.pi / 180.0)
    area_weight = jnp.cos(latitude)
    live_mask = (
        jnp.arange(realization_indices, dtype=jnp.int32)[None, :] < counts[:, None]
    ).astype(jnp.float32)
    gridpoint_weight = area_weight[:, None] * live_mask
    flat_latent = hidden_state.reshape(points, width)
    raveled_prediction = lax.dot_general(
        proj_weight, flat_latent, (((1,), (1,)), ((), ())), preferred_element_type=jnp.float32
    )
    raveled_prediction = raveled_prediction + output_offset_vector[:, None]
    predicted_maps = raveled_prediction.reshape(
        quantity_tally, stored_latitude_lines, realization_indices
    )
    variable_scale = var_weight[:, None, None]
    realization_gaps = predicted_maps[None] - lax.all_gather(
        predicted_maps[None], "member", axis=0, tiled=True
    )
    polarity_totals = jnp.sum(smooth_sign(realization_gaps), axis=0)
    modulus_totals = jnp.sum(smooth_abs(realization_gaps), axis=0)
    field_grad, local_total = finish_field(
        predicted_maps,
        verifying_reanalysis,
        gridpoint_weight[None],
        variable_scale,
        polarity_totals,
        modulus_totals,
        ensemble_members,
    )
    grad_bf = field_grad.astype(jnp.bfloat16).reshape(quantity_tally, points)
    back = lax.dot_general(
        grad_bf, proj_weight, (((0,), (0,)), ((), ())), preferred_element_type=jnp.float32
    )
    latent_grad = (GRAD_SCALE * back).astype(jnp.bfloat16).reshape(hidden_state.shape)
    weight_part = jnp.dot(grad_bf, flat_latent, preferred_element_type=jnp.float32)
    bias_part = jnp.sum(field_grad.reshape(quantity_tally, points), axis=1)
    local_rows = jnp.sum(area_weight * counts.astype(jnp.float32))
    row_total = lax.psum(local_rows, "space")
    weight_sum, bias_sum, total = lax.psum(
        (weight_part, bias_part, local_total), ("member", "space")
    )
    factor = GRAD_SCALE / math.sqrt(ensemble_members * total_rows * realization_indices)
    loss = total / (quantity_tally * row_total)
    return (latent_grad, weight_sum * factor, bias_sum * factor, loss)


def solution(mesh):
    return jax.shard_map(
        per_device,
        mesh=mesh,
        in_specs=(
            P("member", "space", None, None),
            P(),
            P(),
            P(None, "space", None),
            P("space"),
            P(),
        ),
        out_specs=(P("member", "space", None, None), P(), P(), P()),
        check_vma=False,
    )
```

profile of v0, /device:TPU:1, one launch (start us, length us, event | category | flops | bytes accessed | tf_op | source)
XLA Modules:
  0.0 433.0 jit_solution(10631941828009210849)
XLA Ops:
  7.2 0.0 copy-start
  7.2 0.0 all-gather.2.cloned.1.call-start
  7.2 0.9 copy-done
  8.1 3.6 convolution_add_fusion
  11.7 0.0 copy-start.2
  11.7 1.4 broadcast_in_dim_reshape.4
  13.2 0.0 all-gather.2.cloned.1.call-update
  13.2 0.0 all-reduce.3.cloned.1.call-start
  13.3 0.7 multiply_reduce_fusion
  13.9 75.4 %psum.31 = f32[]{:T(128)} all-reduce(f32[]{:T(128)} %multiply_reduce_fusion), channel_id=1, replica_groups=mesh['member'=8,'space'=32] {'space'}, use_global_device_ids=true, to_apply=%region_8.0 | all-reduce | flops 1 | bytes 8 | tf_op jit(solution)/shard_map/psum | solution.py:97
  89.4 0.6 reshape.64
  90.6 0.1 fusion.4
  90.7 70.3 %all-gather.2.cloned.1.call-done = f32[8,100,4,512]{3,2,1,0:T(4,128)} async-done(((f32[1,100,4,512]{3,2,1,0:T(4,128)}), f32[8,100,4,512]{3,2,1,0:T(4,128)}) %all-gather.2.cloned.1.call-update) | async-done | bytes 6553616 | tf_op jit(solution)/shard_map/all_gather | solution.py:75
  161.0 11.0 %add_reduce_fusion = (f32[100,4,512]{2,1,0:T(4,128)S(1)}, f32[100,4,512]{2,1,0:T(4,128)S(1)}) fusion(f32[8,100,4,512]{3,2,1,0:T(4,128)} %all-gather.2.cloned.1.call-done, f32[100,4,512]{2,1,0:T(4,128)S(1)} %reshape.64), kind=kLoop, calls=%fused_computation.1 | loop fusion | flops 11059200 | bytes 9011200 | tf_op jit(solution)/shard_map/reduce_sum | solution.py:79
  172.1 2.7 fusion.5
  174.8 0.2 pad
  175.0 0.1 copy.10
  175.1 1.6 fusion.6
  176.7 3.3 multiply_convert_fusion
  180.0 0.0 all-reduce.3.cloned.1.call-update
  180.0 74.5 %all-reduce = (f32[100]{0:T(128)S(1)}, f32[]{:T(128)}) all-reduce(f32[100]{0:T(128)S(1)} %get-tuple-element.8, f32[]{:T(128)} %get-tuple-element.10), channel_id=1, replica_groups=mesh['member'=8,'space'=32] {'member','space'}, use_global_device_ids=true, to_apply=%region_3.0 | all-reduce | flops 101 | bytes 808 | tf_op jit(solution)/shard_map/psum | solution.py:98
  255.2 0.5 broadcast_multiply_fusion.1
  255.7 167.6 %all-reduce.3.cloned.1.call-done = f32[100,1024]{1,0:T(8,128)} async-done(((f32[100,1024]{1,0:T(8,128)}), f32[100,1024]{1,0:T(8,128)}) %all-reduce.3.cloned.1.call-update) | async-done | bytes 409616 | tf_op jit(solution)/shard_map/psum | solution.py:98
  423.3 1.8 broadcast_multiply_fusion
  (8 shorter events, 0.1 us)
Async XLA Ops:
  7.2 0.9 copy-start
  7.2 6.1 %copy-start.4 = (s32[4]{0:T(128)S(1)}, s32[4]{0:T(128)}, u32[]{:S(2)}) copy-start(s32[4]{0:T(128)} %param.10) | copy-start | bytes 52
  7.2 153.8 %all-gather.2.cloned.1.call-start = ((), (), s32[]{:S(2)}) async-start(), calls=%async_computation | async-start | bytes 7372800 | tf_op jit(solution)/shard_map/all_gather | solution.py:75
  11.7 160.4 %copy-start.2 = (f32[100,4,512]{2,1,0:T(4,128)S(1)}, f32[100,4,512]{2,1,0:T(4,128)}, u32[]{:S(2)}) copy-start(f32[100,4,512]{2,1,0:T(4,128)} %param.9) | copy-start | bytes 2457604
  11.7 160.4 %copy-start.3 = (f32[100]{0:T(128)S(1)}, f32[100]{0:T(128)}, u32[]{:S(2)}) copy-start(f32[100]{0:T(128)} %param.11) | copy-start | bytes 1204
  13.2 410.1 %all-reduce.3.cloned.1.call-start = ((), (), s32[]{:S(2)}) async-start(), calls=%async_computation.1 | async-start | bytes 851968 | tf_op jit(solution)/shard_map/psum | solution.py:98
  161.0 14.0 %copy-start.1 = (bf16[1,4,512,1024]{3,2,1,0:T(8,128)(2,1)S(1)}, bf16[1,4,512,1024]{3,2,1,0:T(8,128)(2,1)}, u32[]{:S(2)}) copy-start(bf16[1,4,512,1024]{3,2,1,0:T(8,128)(2,1)} %param.6) | copy-start | bytes 12582916
Sparse Core Ops, SparseCore 0:
  13.3 147.6 all-gather.1
  180.1 243.1 all-reduce.2
where the time goes:
time: 434 us; the launch traced here: 433 us
  waiting for transfers between devices  238 us (55%)
  blocking collectives  150 us (35%)
  other arithmetic  16.8 us (4%)
  between operations  16.6 us (4%)
  matrix products  8.49 us (2%)
    psum x1, waiting for transfers between devices, per_device(): lax.psum((weight_part, bias_part, local_total), ('member', 'space'))  168 us
    psum x1, blocking collectives, per_device(): row_total = lax.psum(local_rows, 'space')  75.4 us
    psum x1, blocking collectives, per_device(): lax.psum((weight_part, bias_part, local_total), ('member', 'space'))  74.5 us
    all_gather x1, waiting for transfers between devices, per_device(): lax.all_gather(predicted_maps[None], 'member', axis=0, tiled=True)  70.3 us
    reduce_sum x1, other arithmetic, per_device(): modulus_totals = jnp.sum(smooth_abs(realization_gaps), axis=0)  11 us
  transfers between devices with their start and end apart: 2, of which 2 were waited for; matrix products, arithmetic and copies ran while one was open for 0% of the time, Pallas kernels for 0%

commit v1 on v0

v1 whole, which is shorter than its diff:
```python
import math

import numpy as np

import jax
import jax.numpy as jnp
from jax import lax
from jax.experimental import pallas as pl
from jax.experimental.pallas import tpu as pltpu
from jax.sharding import PartitionSpec as P

SMOOTHING = 0.05
FAIRNESS = 0.95
GRAD_SCALE = 16.0
LATITUDE_SPAN = 80.0

V = 100
VP = 104
D = 1024
ROWS = 4
CAP = 512
POINTS = ROWS * CAP
BLOCK = 256
NB = 8
TILES = VP // 8
GP = 112
CHUNKS = ((0, 32), (32, 32), (64, 40))
SENT = (32, 32, 40)
GROUPS = ((0, 64), (64, 40))
NC = len(CHUNKS)
MESH = pl.DeviceIdType.MESH
F32 = jnp.float32
EPS2 = SMOOTHING * SMOOTHING
COEFF = FAIRNESS / (NB * (NB - 1)) + (1.0 - FAIRNESS) / (NB * NB)


def column(row):
    n = row.shape[1]
    here = lax.broadcasted_iota(jnp.int32, (VP, n), 0) == lax.broadcasted_iota(
        jnp.int32, (VP, n), 1
    )
    return jnp.sum(jnp.where(here, jnp.broadcast_to(row, (VP, n)), 0.0), axis=1, keepdims=True)


def exchange_kernel(
    counts_ref,
    area_ref,
    offset_ref,
    scale_ref,
    weight_hbm,
    hidden_hbm,
    truth_hbm,
    latent_ref,
    sums_ref,
    weight,
    hbuf,
    truth,
    field,
    met,
    signs,
    back,
    obs,
    grad,
    loss_acc,
    bias_acc,
    offset_col,
    scale_col,
    part,
    part_in,
    plane,
    y_in,
    z_out,
    z_in,
    own_all,
    out_in,
    load_sem,
    side_sem,
    fwd_send,
    fwd_recv,
    ret_send,
    ret_recv,
    part_send,
    part_recv,
    y_send,
    y_recv,
    z_send,
    z_recv,
    row_send,
    row_recv,
    out_send,
    out_recv,
):
    member = lax.axis_index("member")
    space = lax.axis_index("space")
    y, z_hi = lax.div(member, 2), lax.rem(member, 2)
    z_lo, q = lax.div(space, 8), lax.rem(space, 8)
    z = z_hi * 4 + z_lo

    def at(yy, zz):
        return (yy * 2 + lax.div(zz, 4), lax.rem(zz, 4) * 8 + q)

    def beside(j):
        return (member, z_lo * 8 + j)

    def load(t):
        b = lax.rem(member + t, NB)
        rows = pl.ds(pl.multiple_of(b * BLOCK, BLOCK), BLOCK)
        return pltpu.make_async_copy(hidden_hbm.at[rows], hbuf.at[rows], load_sem.at[t])

    load_weight = pltpu.make_async_copy(weight_hbm, weight, side_sem.at[0])
    load_weight.start()
    for t in range(NB):
        load(t).start()
    load_truth = pltpu.make_async_copy(truth_hbm, truth.at[pl.ds(0, V)], side_sem.at[1])
    load_truth.start()

    met[:, V:VP, :] = jnp.zeros((NB, VP - V, BLOCK), F32)
    back[:, V:VP, :] = jnp.zeros((NB, VP - V, BLOCK), F32)

    barrier = pltpu.get_barrier_semaphore()

    def greet(device):
        pl.semaphore_signal(barrier, inc=1, device_id=device, device_id_type=MESH)

    @pl.loop(1, 8)
    def _(t):
        greet(beside(lax.rem(q + t, 8)))
        greet(at(y, lax.rem(z + t, 8)))

    @pl.loop(1, ROWS)
    def _(t):
        for step in (0, 2, 6):
            greet(at(lax.rem(y + t, ROWS), lax.rem(z + step, 8)))

    offset_col[...] = jnp.broadcast_to(column(offset_ref[...]), (VP, 128))
    scale_col[...] = jnp.broadcast_to(column(scale_ref[...]), (VP, 128))
    loss_acc[...] = jnp.zeros_like(loss_acc)
    bias_acc[...] = jnp.zeros_like(bias_acc)
    field[:, V:VP, :] = jnp.zeros((NB, VP - V, BLOCK), F32)
    truth[V:VP] = jnp.zeros((VP - V, ROWS, CAP), F32)

    lanes = lax.broadcasted_iota(jnp.int32, (1, BLOCK), 1)

    def live(b):
        return lanes + lax.rem(b, 2) * BLOCK < counts_ref[lax.div(b, 2)]

    def send_forecast(c, b):
        v0, n = CHUNKS[c][0], SENT[c]
        zz = lax.rem(z_lo + 2 + 4 * lax.rem(b, 2), 8)
        return pltpu.make_async_remote_copy(
            src_ref=field.at[b, pl.ds(v0, n)],
            dst_ref=met.at[member, pl.ds(v0, n)],
            send_sem=fwd_send.at[c, b],
            recv_sem=fwd_recv.at[c],
            device_id=at(lax.div(b, 2), zz),
            device_id_type=MESH,
        )

    def send_forecasts(c):
        @pl.loop(0, NB)
        def _(t):
            send_forecast(c, lax.rem(member + t, NB)).start()

    @pl.loop(0, NB)
    def _(t):
        load(t).wait()

        @pl.when(t == 0)
        def _():
            load_weight.wait()

        b = lax.rem(member + t, NB)
        rows = pl.ds(pl.multiple_of(b * BLOCK, BLOCK), BLOCK)
        product = lax.dot_general(
            weight[...], hbuf[rows, :], (((1,), (1,)), ((), ())), preferred_element_type=F32
        )
        forecast = product + offset_col[0:V, 0:1]
        field[b, 0:V, :] = jnp.where(live(b), forecast, 0.0)

        @pl.when(t == 0)
        def _():
            pl.semaphore_wait(barrier, 23)

        send_forecast(0, b).start()

    for c in range(1, NC):
        send_forecasts(c)

    load_truth.wait()

    @pl.loop(0, TILES)
    def _(i):
        at_v = pl.ds(pl.multiple_of(i * 8, 8), 8)
        for b in range(NB):
            r, half = b // 2, b % 2
            point_weight = jnp.where(live(b), area_ref[space * ROWS + r], 0.0) * (1.0 / NB)
            factor = point_weight * scale_col[at_v, 0:1]
            gap = field[b, at_v, :] - truth[at_v, r, half * BLOCK : (half + 1) * BLOCK]
            square = gap * gap + EPS2
            inverse = lax.rsqrt(square)
            obs[b, at_v, :] = factor * (gap * inverse)
            misfit = factor * (square * inverse - SMOOTHING)
            loss_acc[at_v, :] += misfit[:, 0:128] + misfit[:, 128:256]

    z_from = lax.rem(z + 2, 4)
    block_here = y * 2 + lax.div(lax.rem(z - z_from - 2 + 16, 8), 4)
    space_from = z_from * 8 + q
    area_here = area_ref[space_from * ROWS + y]

    def send_sign(c, m):
        v0, n = CHUNKS[c][0], SENT[c]
        return pltpu.make_async_remote_copy(
            src_ref=signs.at[m, pl.ds(v0, n)],
            dst_ref=back.at[block_here, pl.ds(v0, n)],
            send_sem=ret_send.at[c, m],
            recv_sem=ret_recv.at[c],
            device_id=(m, space_from),
            device_id_type=MESH,
        )

    def pairs(c):
        v0, n = CHUNKS[c]
        arrived = met.at[:, pl.ds(v0, SENT[c])]
        pltpu.make_async_copy(arrived, arrived, fwd_recv.at[c]).wait()

        @pl.loop(0, n // 8)
        def _(i):
            at_v = pl.ds(pl.multiple_of(v0 + i * 8, 8), 8)
            values = [met[m, at_v, :] for m in range(NB)]
            sums = [None] * NB
            roots = None
            for m in range(NB):
                for k in range(m + 1, NB):
                    gap = values[m] - values[k]
                    square = gap * gap + EPS2
                    inverse = lax.rsqrt(square)
                    sign = gap * inverse
                    root = square * inverse
                    roots = root if roots is None else roots + root
                    sums[m] = sign if sums[m] is None else sums[m] + sign
                    sums[k] = -sign if sums[k] is None else sums[k] - sign
            for m in range(NB):
                signs[m, at_v, :] = sums[m]
            spread = roots - (NB * (NB - 1) // 2) * SMOOTHING
            spread = (-COEFF * area_here) * scale_col[at_v, 0:1] * spread
            loss_acc[at_v, :] += spread[:, 0:128] + spread[:, 128:256]

        @pl.loop(0, NB)
        def _(t):
            send_sign(c, lax.rem(member + t, NB)).start()

    lane = lax.broadcasted_iota(jnp.int32, (1, 128), 1)
    sub = lax.broadcasted_iota(jnp.int32, (8, 128), 0)

    def extras():
        bias = jnp.sum(bias_acc[...], axis=1, keepdims=True)
        eye = lax.broadcasted_iota(jnp.int32, (VP, 128), 0) == lax.broadcasted_iota(
            jnp.int32, (VP, 128), 1
        )
        extra = jnp.sum(jnp.where(eye, bias, 0.0), axis=0, keepdims=True)
        loss_here = jnp.sum(jnp.sum(loss_acc[...], axis=0, keepdims=True), axis=1, keepdims=True)
        points_here = jnp.float32(0.0)
        for r in range(ROWS):
            points_here += area_ref[space * ROWS + r] * counts_ref[r].astype(F32)
        extra = jnp.where(lane < V, extra, 0.0)
        extra = jnp.where(lane == V, loss_here, extra)
        extra = jnp.where(lane == V + 1, points_here, extra)
        part[0, 96:VP, :] = jnp.where(sub == V - 96, extra, part[0, 96:VP, :])

    def gradient(c):
        v0, n = CHUNKS[c]
        arrived = back.at[:, pl.ds(v0, SENT[c])]
        pltpu.make_async_copy(arrived, arrived, ret_recv.at[c]).wait()
        padded = (n + 15) // 16 * 16

        @pl.loop(0, NB)
        def _(b):
            points = pl.ds(pl.multiple_of(b * BLOCK, BLOCK), BLOCK)
            area = area_ref[space * ROWS + lax.div(b, 2)]
            point_weight = jnp.where(live(b), area * COEFF, 0.0)
            factor = point_weight * scale_col[v0 : v0 + n, 0:1]
            value = obs[b, v0 : v0 + n, :] - factor * back[b, v0 : v0 + n, :]
            bias_acc[v0 : v0 + n, :] += value[:, 0:128] + value[:, 128:256]
            if padded > n:
                value = jnp.concatenate([value, jnp.zeros((padded - n, BLOCK), F32)], axis=0)
            grad[v0 : v0 + padded, points] = value.astype(jnp.bfloat16)

        @pl.loop(0, 4)
        def _(j):
            piece = jnp.dot(
                grad[v0 : v0 + padded, :],
                hbuf[:, pl.ds(pl.multiple_of(j * 256, 256), 256)],
                preferred_element_type=F32,
            )
            part[2 * j, v0 : v0 + n, :] = piece[0:n, 0:128]
            part[2 * j + 1, v0 : v0 + n, :] = piece[0:n, 128:256]

    def tiles(g):
        first, n = GROUPS[g]
        return first // 8, (first + n) // 8

    def send_part(g, t):
        first, n = GROUPS[g]
        j = lax.rem(q + t, 8)
        return pltpu.make_async_remote_copy(
            src_ref=part.at[j, pl.ds(first, n)],
            dst_ref=part_in.at[t - 1, pl.ds(first, n)],
            send_sem=part_send.at[g, t - 1],
            recv_sem=part_recv.at[g],
            device_id=beside(j),
            device_id_type=MESH,
        )

    def send_plane(g, t):
        yy = lax.rem(y + t, ROWS)
        return pltpu.make_async_remote_copy(
            src_ref=plane.at[g, yy],
            dst_ref=y_in.at[g, y],
            send_sem=y_send.at[g, t - 1],
            recv_sem=y_recv.at[g],
            device_id=at(yy, z),
            device_id_type=MESH,
        )

    def send_across(g, t):
        return pltpu.make_async_remote_copy(
            src_ref=z_out.at[g],
            dst_ref=z_in.at[g, z],
            send_sem=z_send.at[g, t - 1],
            recv_sem=z_recv.at[g],
            device_id=at(y, lax.rem(z + t, 8)),
            device_id_type=MESH,
        )

    def send_row(g, t):
        block = own_all.at[pl.ds(2 * y, 2) if g == 0 else pl.ds(8 + y, 1)]
        return pltpu.make_async_remote_copy(
            src_ref=block,
            dst_ref=block,
            send_sem=row_send.at[g, t - 1],
            recv_sem=row_recv.at[g],
            device_id=at(lax.rem(y + t, ROWS), z),
            device_id_type=MESH,
        )

    def send_out(g, t):
        first, end = tiles(g)
        block = pl.ds(first, end - first)
        return pltpu.make_async_remote_copy(
            src_ref=own_all.at[block],
            dst_ref=out_in.at[t, block],
            send_sem=out_send.at[g, t - 1],
            recv_sem=out_recv.at[g],
            device_id=beside(lax.rem(q + t, 8)),
            device_id_type=MESH,
        )

    def send_all(send, g, number):
        @pl.loop(1, number)
        def _(t):
            send(g, t).start()

    def arrive(ref, sem):
        pltpu.make_async_copy(ref, ref, sem).wait()

    def sum_beside(g):
        first, n = GROUPS[g]
        arrive(part_in.at[:, pl.ds(first, n)], part_recv.at[g])

        def column_sum(o):
            at_v = pl.ds(pl.multiple_of(o * 8, 8), 8)
            value = part[q, at_v, :]
            for t in range(7):
                value += part_in[t, at_v, :]
            return value

        if g == 0:

            @pl.loop(0, ROWS)
            def _(yy):
                for i in range(2):
                    plane[g, yy, i] = column_sum(2 * yy + i)
        else:
            last = column_sum(TILES - 1)

            @pl.loop(0, ROWS)
            def _(yy):
                plane[g, yy, 0] = column_sum(8 + yy)
                plane[g, yy, 1] = last

        send_all(send_plane, g, ROWS)
        y_in[g, y] = plane[g, y]

    def sum_plane(g):
        arrive(y_in.at[g, pl.ds(0, 3)], y_recv.at[g])
        value = y_in[g, 0]
        for yy in range(1, ROWS):
            value += y_in[g, yy]
        z_out[g] = value
        send_all(send_across, g, 8)
        z_in[g, z] = value

    def sum_across(g):
        arrive(z_in.at[g, pl.ds(0, 7)], z_recv.at[g])
        value = z_in[g, 0]
        for zz in range(1, 8):
            value += z_in[g, zz]
        if g == 0:
            own_all[pl.ds(2 * y, 2)] = value
        else:
            own_all[8 + y] = value[0]
            own_all[TILES - 1] = value[1]
        send_all(send_row, g, ROWS)

    def spread_out(g):
        first, end = tiles(g)
        arrive(own_all.at[pl.ds(0, 6 if g == 0 else 3)], row_recv.at[g])
        send_all(send_out, g, 8)
        out_in[0, first:end] = own_all[first:end]

    def collect(g):
        first, end = tiles(g)
        arrive(out_in.at[pl.ds(1, 7), pl.ds(first, end - first)], out_recv.at[g])

        @pl.loop(0, 8)
        def _(t):
            cols = pl.ds(pl.multiple_of(lax.rem(q - t + 8, 8) * 128, 128), 128)
            for o in range(first, end):
                sums_ref[o * 8 : (o + 1) * 8, cols] = out_in[t, o]

    def latent(first, end):
        @pl.loop(first, end)
        def _(b):
            points = pl.ds(pl.multiple_of(b * BLOCK, BLOCK), BLOCK)
            value = lax.dot_general(
                grad[0:V, points], weight[...], (((0,), (0,)), ((), ())), preferred_element_type=F32
            )
            latent_ref[points, :] = (GRAD_SCALE * value).astype(jnp.bfloat16)

    for c in range(NC):
        pairs(c)
    gradient(0)
    gradient(1)
    send_all(send_part, 0, 8)
    sum_beside(0)
    sum_plane(0)
    gradient(2)
    extras()
    send_all(send_part, 1, 8)
    sum_across(0)
    latent(0, 2)
    sum_beside(1)
    spread_out(0)
    latent(2, 4)
    sum_plane(1)
    latent(4, 6)
    sum_across(1)
    collect(0)
    latent(6, 8)
    spread_out(1)
    collect(1)

    for c in range(NC):

        @pl.loop(0, NB)
        def _(b):
            send_forecast(c, b).wait_send()
            send_sign(c, b).wait_send()

    for g in range(len(GROUPS)):

        @pl.loop(1, 8)
        def _(t):
            send_part(g, t).wait_send()
            send_across(g, t).wait_send()
            send_out(g, t).wait_send()

        @pl.loop(1, ROWS)
        def _(t):
            send_plane(g, t).wait_send()
            send_row(g, t).wait_send()


def finish_kernel(factor, latent, sums, latent_hbm, wgrad_hbm, bias_ref, loss_ref, wgrad, sem):
    store_latent = pltpu.make_async_copy(latent, latent_hbm, sem.at[0])
    store_latent.start()
    wgrad[...] = sums[0:V, :] * factor
    store_wgrad = pltpu.make_async_copy(wgrad, wgrad_hbm, sem.at[1])
    store_wgrad.start()
    extra = sums[V : V + 1, 0:128]
    lane = lax.broadcasted_iota(jnp.int32, (1, 128), 1)
    total = jnp.sum(jnp.where(lane == V, extra, 0.0), axis=1, keepdims=True)
    points = jnp.sum(jnp.where(lane == V + 1, extra, 0.0), axis=1, keepdims=True)
    bias_ref[...] = extra[:, 0:V] * factor
    loss_ref[...] = total / (V * (points * (1.0 / NB)))
    store_wgrad.wait()
    store_latent.wait()


def per_device(hidden_state, proj_weight, offset, truth, counts, var_weight, total_rows):
    latitude = (np.arange(total_rows) + 0.5) * (LATITUDE_SPAN / total_rows) * (math.pi / 180.0)
    area = jnp.asarray(np.cos(latitude), dtype=F32)
    vmem = pl.BlockSpec(memory_space=pltpu.VMEM)
    smem = pl.BlockSpec(memory_space=pltpu.SMEM)
    hbm = pl.BlockSpec(memory_space=pltpu.HBM)
    dma = pltpu.SemaphoreType.DMA
    bf16 = jnp.bfloat16
    blocks = pltpu.VMEM((NB, VP, BLOCK), F32)
    ng = len(GROUPS)
    latent, sums = pl.pallas_call(
        exchange_kernel,
        out_shape=(
            pltpu.VMEM((POINTS, D), bf16),
            pltpu.VMEM((VP, D), F32),
        ),
        in_specs=[smem, smem, vmem, vmem, hbm, hbm, hbm],
        out_specs=(vmem, vmem),
        scratch_shapes=[
            pltpu.VMEM((V, D), bf16),
            pltpu.VMEM((POINTS, D), bf16),
            pltpu.VMEM((VP, ROWS, CAP), F32),
            blocks,
            blocks,
            blocks,
            blocks,
            blocks,
            pltpu.VMEM((GP, POINTS), bf16),
            pltpu.VMEM((VP, 128), F32),
            pltpu.VMEM((VP, 128), F32),
            pltpu.VMEM((VP, 128), F32),
            pltpu.VMEM((VP, 128), F32),
            pltpu.VMEM((8, VP, 128), F32),
            pltpu.VMEM((7, VP, 128), F32),
            pltpu.VMEM((ng, ROWS, 2, 8, 128), F32),
            pltpu.VMEM((ng, ROWS, 2, 8, 128), F32),
            pltpu.VMEM((ng, 2, 8, 128), F32),
            pltpu.VMEM((ng, 8, 2, 8, 128), F32),
            pltpu.VMEM((TILES, 8, 128), F32),
            pltpu.VMEM((8, TILES, 8, 128), F32),
            dma((NB,)),
            dma((2,)),
            dma((NC, NB)),
            dma((NC,)),
            dma((NC, NB)),
            dma((NC,)),
            dma((ng, 7)),
            dma((ng,)),
            dma((ng, 3)),
            dma((ng,)),
            dma((ng, 7)),
            dma((ng,)),
            dma((ng, 3)),
            dma((ng,)),
            dma((ng, 7)),
            dma((ng,)),
        ],
        compiler_params=pltpu.CompilerParams(
            collective_id=0, has_side_effects=True, vmem_limit_bytes=59 * 1024 * 1024
        ),
        cost_estimate=pl.CostEstimate(
            flops=4 * V * POINTS * D, bytes_accessed=5_000_000, transcendentals=8_000_000
        ),
    )(
        counts,
        area,
        offset.reshape(1, V),
        var_weight.reshape(1, V),
        proj_weight,
        hidden_state.reshape(POINTS, D),
        truth,
    )
    factor = GRAD_SCALE / math.sqrt(NB * total_rows * CAP)
    latent, wgrad, bias, loss = pl.pallas_call(
        lambda *refs: finish_kernel(factor, *refs),
        out_shape=(
            jax.ShapeDtypeStruct((POINTS, D), bf16),
            jax.ShapeDtypeStruct((V, D), F32),
            jax.ShapeDtypeStruct((1, V), F32),
            jax.ShapeDtypeStruct((1, 1), F32),
        ),
        in_specs=[vmem, vmem],
        out_specs=(hbm, hbm, vmem, vmem),
        scratch_shapes=[pltpu.VMEM((V, D), F32), dma((2,))],
        compiler_params=pltpu.CompilerParams(vmem_limit_bytes=16 * 1024 * 1024),
        cost_estimate=pl.CostEstimate(flops=V * D, bytes_accessed=5_000_000, transcendentals=0),
    )(latent, sums)
    return latent.reshape(hidden_state.shape), wgrad, bias.reshape(V), loss.reshape(())


def solution(mesh):
    total_rows = ROWS * mesh.shape["space"]

    def step(*args):
        return per_device(*args, total_rows)

    return jax.shard_map(
        step,
        mesh=mesh,
        in_specs=(
            P("member", "space", None, None),
            P(),
            P(),
            P(None, "space", None),
            P("space"),
            P(),
        ),
        out_specs=(P("member", "space", None, None), P(), P(), P()),
        check_vma=False,
    )
```

time: 434 us -> 85.6 us (0.20)
  waiting for transfers between devices: 238 us -> 0 us
  blocking collectives: 150 us -> 0 us
  Pallas kernels: 0 us -> 84.8 us
  other arithmetic: 16.8 us -> 0 us
  between operations: 16.6 us -> 0.64 us
  matrix products: 8.49 us -> 0 us
    psum x1 -> x0, waiting for transfers between devices: 168 us -> none  [per_device(): lax.psum((weight_part, bias_part, local_total), ('member', 'space'))]
    psum x2 -> x0, blocking collectives: 150 us -> none  [the longest x1 75.4 us: per_device(): row_total = lax.psum(local_rows, 'space')]
    pallas_call x0 -> x2, Pallas kernels: none -> 84.8 us  [the longest x1 82.2 us: per_device(): pl.pallas_call(exchange_kernel, out_shape=(pltpu.VMEM((POINTS, D), bf16),...]
    all_gather x1 -> x0, waiting for transfers between devices: 70.3 us -> none  [per_device(): lax.all_gather(predicted_maps[None], 'member', axis=0, tiled=True)]
    reduce_sum x3 -> x0, other arithmetic: 14.4 us -> none  [the longest x1 11 us: per_device(): modulus_totals = jnp.sum(smooth_abs(realization_gaps), axis=0)]
    dot_general x3 -> x0, matrix products: 8.49 us -> none  [the longest x1 3.61 us: per_device(): lax.dot_general(proj_weight, flat_latent, (((1,), (1,)), ((), ())), prefe...]
  transfers between devices with their start and end apart: 2 -> 0, of which waited for: 2 -> 0; matrix products, arithmetic and copies ran while one was open for 0% -> 0% of each run, Pallas kernels for 0% -> 0%
where the time goes in v1:
time: 85.6 us; the launch traced here: 85.5 us
  Pallas kernels  84.8 us (99%)
    pallas_call x1, Pallas kernels, per_device(): pl.pallas_call(exchange_kernel, out_shape=(pltpu.VMEM((POINTS, D), bf16),...  82.2 us
    pallas_call x1, Pallas kernels, per_device(): pl.pallas_call(lambda *refs: finish_kernel(factor, *refs), out_shape=(jax...  2.67 us

profile of v1, /device:TPU:1, one launch (start us, length us, event | category | flops | bytes accessed | tf_op | source)
XLA Modules:
  0.0 85.5 jit_solution(7694883499353836251)
XLA Ops:
  0.6 82.2 %shard_map.102 = (bf16[2048,1024]{1,0:T(8,128)(2,1)S(1)}, f32[104,1024]{1,0:T(8,128)S(1)}) custom-call(s32[4]{0:T(128)} %counts_ref.1, f32[128]{0:T(128)} %constant.2.clone.area_ref, f32[1,100]{1,0:T(1,128)} %bitcast.8, f32[1,100]{1,0:T(1,128)} %bitcast.9, bf16[100,1024]{1,0:T(8,128)(2,1)} %weight_hbm.1, bf16[2048,1024]{1,0:T(8,128)(2,1)} %bitcast.6, ...), custom_call_target="tpu_custom_call" | custom-call | flops 838860800 | bytes 5000000 | tf_op jit(solution)/shard_map/pallas_call | solution.py:510
  82.8 2.7 %shard_map.103 = (bf16[2048,1024]{1,0:T(8,128)(2,1)}, f32[100,1024]{1,0:T(8,128)}, f32[1,100]{1,0:T(1,128)}, f32[1,1]{1,0:T(1,128)}) custom-call(bf16[2048,1024]{1,0:T(8,128)(2,1)S(1)} %get-tuple-element.10.refs_0_, f32[104,1024]{1,0:T(8,128)S(1)} %get-tuple-element.11.refs_1_), custom_call_target="tpu_custom_call" | custom-call | flops 102400 | bytes 5000000 | tf_op jit(solution)/shard_map/pallas_call | solution.py:573

commit v2 on v1

v2 whole, which is shorter than its diff:
```python
import math

import numpy as np

import jax
import jax.numpy as jnp
from jax import lax
from jax.experimental import pallas as pl
from jax.experimental.pallas import tpu as pltpu
from jax.sharding import PartitionSpec as P

SMOOTHING = 0.05
FAIRNESS = 0.95
GRAD_SCALE = 16.0
LATITUDE_SPAN = 80.0

V = 100
VP = 104
D = 1024
ROWS = 4
CAP = 512
POINTS = ROWS * CAP
BLOCK = 256
NB = 8
TILES = VP // 8
GP = 112
CHUNKS = ((0, 16), (16, 32), (48, 32), (80, 16), (96, 8))
SENT = (16, 32, 32, 16, 4)
NC = len(CHUNKS)
MESH = pl.DeviceIdType.MESH
F32 = jnp.float32
EPS2 = SMOOTHING * SMOOTHING
COEFF = FAIRNESS / (NB * (NB - 1)) + (1.0 - FAIRNESS) / (NB * NB)


def column(row):
    n = row.shape[1]
    here = lax.broadcasted_iota(jnp.int32, (VP, n), 0) == lax.broadcasted_iota(
        jnp.int32, (VP, n), 1
    )
    return jnp.sum(jnp.where(here, jnp.broadcast_to(row, (VP, n)), 0.0), axis=1, keepdims=True)


def exchange_kernel(
    counts_ref,
    area_ref,
    offset_ref,
    scale_ref,
    weight_hbm,
    hidden_hbm,
    truth_hbm,
    latent_ref,
    sums_ref,
    weight,
    hbuf,
    truth,
    field,
    met,
    signs,
    back,
    obs,
    grad,
    loss_acc,
    bias_acc,
    offset_col,
    scale_col,
    part,
    part_in,
    plane,
    plane_in,
    own_all,
    out_in,
    load_sem,
    side_sem,
    fwd_send,
    fwd_recv,
    ret_send,
    ret_recv,
    rs1_send,
    rs1_recv,
    rs2_send,
    rs2_recv,
    ag2_send,
    ag2_recv,
    ag1_send,
    ag1_recv,
):
    member = lax.axis_index("member")
    space = lax.axis_index("space")
    y, z_hi = lax.div(member, 2), lax.rem(member, 2)
    z_lo, q = lax.div(space, 8), lax.rem(space, 8)
    core = lax.rem(q, 2)
    z = z_hi * 4 + z_lo
    rank = y * 8 + z

    def at(yy, zz):
        return (yy * 2 + lax.div(zz, 4), lax.rem(zz, 4) * 8 + q)

    def at_rank(p):
        return at(lax.div(p, 8), lax.rem(p, 8))

    def beside(j):
        return (member, z_lo * 8 + j)

    def load(t):
        b = lax.rem(member + t, NB)
        rows = pl.ds(pl.multiple_of(b * BLOCK, BLOCK), BLOCK)
        return pltpu.make_async_copy(hidden_hbm.at[rows], hbuf.at[rows], load_sem.at[t - 1])

    load_weight = pltpu.make_async_copy(weight_hbm, weight, side_sem.at[0])
    load_weight.start()
    for t in range(1, NB + 1):
        load(t).start()
    load_truth = pltpu.make_async_copy(truth_hbm, truth, side_sem.at[1])
    load_truth.start()

    met[:, V:VP, :] = jnp.zeros((NB, VP - V, BLOCK), F32)
    back[:, V:VP, :] = jnp.zeros((NB, VP - V, BLOCK), F32)

    barrier = pltpu.get_barrier_semaphore()

    @pl.loop(1, 8)
    def _(t):
        pl.semaphore_signal(
            barrier, inc=1, device_id=beside(lax.rem(q + t, 8)), device_id_type=MESH
        )

    @pl.loop(1, 32)
    def _(t):
        pl.semaphore_signal(
            barrier, inc=1, device_id=at_rank(lax.rem(rank + t, 32)), device_id_type=MESH
        )

    offset_col[...] = jnp.broadcast_to(column(offset_ref[...]), (VP, 128))
    scale_col[...] = jnp.broadcast_to(column(scale_ref[...]), (VP, 128))
    loss_acc[...] = jnp.zeros_like(loss_acc)
    bias_acc[...] = jnp.zeros_like(bias_acc)
    obs[:, 96:VP, :] = jnp.zeros((NB, VP - 96, BLOCK), F32)

    lanes = lax.broadcasted_iota(jnp.int32, (1, BLOCK), 1)

    def live(b):
        return lanes + lax.rem(b, 2) * BLOCK < counts_ref[lax.div(b, 2)]

    def send_forecast(c, b):
        v0, n = CHUNKS[c][0], SENT[c]
        return pltpu.make_async_remote_copy(
            src_ref=field.at[b, pl.ds(v0, n)],
            dst_ref=met.at[member, pl.ds(v0, n)],
            send_sem=fwd_send.at[c, b],
            recv_sem=fwd_recv.at[c],
            device_id=(b, space),
            device_id_type=MESH,
        )

    def keep_forecast(c):
        v0, n = CHUNKS[c][0], SENT[c]
        return pltpu.make_async_copy(
            field.at[member, pl.ds(v0, n)], met.at[member, pl.ds(v0, n)], fwd_recv.at[c]
        )

    def send_forecasts(c):
        @pl.loop(1, NB)
        def _(t):
            send_forecast(c, lax.rem(member + t, NB)).start()

        keep_forecast(c).start()

    for t in range(1, NB + 1):
        load(t).wait()
        if t == 1:
            load_weight.wait()
        b = lax.rem(member + t, NB)
        rows = pl.ds(pl.multiple_of(b * BLOCK, BLOCK), BLOCK)
        product = lax.dot_general(
            weight[...], hbuf[rows, :], (((1,), (1,)), ((), ())), preferred_element_type=F32
        )
        forecast = product + offset_col[0:V, 0:1]
        field[b, 0:V, :] = jnp.where(live(b), forecast, 0.0)
        if t == 1:
            pl.semaphore_wait(barrier, 38)
        for c in range(2):
            if t < NB:
                send_forecast(c, b).start()
            else:
                keep_forecast(c).start()

    load_truth.wait()
    for b in range(NB):
        r, half = b // 2, b % 2
        point_weight = jnp.where(live(b), area_ref[space * ROWS + r], 0.0) * (1.0 / NB)
        factor = point_weight * scale_col[0:V, 0:1]
        gap = field[b, 0:V, :] - truth[:, r, half * BLOCK : (half + 1) * BLOCK]
        square = gap * gap + EPS2
        inverse = lax.rsqrt(square)
        obs[b, 0:V, :] = factor * (gap * inverse)
        misfit = factor * (square * inverse - SMOOTHING)
        loss_acc[0:V, :] += misfit[:, 0:128] + misfit[:, 128:256]

    area_here = area_ref[space * ROWS + y]

    def send_sign(c, m):
        v0, n = CHUNKS[c][0], SENT[c]
        return pltpu.make_async_remote_copy(
            src_ref=signs.at[m, pl.ds(v0, n)],
            dst_ref=back.at[member, pl.ds(v0, n)],
            send_sem=ret_send.at[c, m],
            recv_sem=ret_recv.at[c],
            device_id=(m, space),
            device_id_type=MESH,
        )

    def keep_sign(c):
        v0, n = CHUNKS[c][0], SENT[c]
        return pltpu.make_async_copy(
            signs.at[member, pl.ds(v0, n)], back.at[member, pl.ds(v0, n)], ret_recv.at[c]
        )

    def pairs(c):
        v0, n = CHUNKS[c]
        arrived = met.at[:, pl.ds(v0, SENT[c])]
        pltpu.make_async_copy(arrived, arrived, fwd_recv.at[c]).wait()

        @pl.loop(0, n // 8)
        def _(i):
            at_v = pl.ds(pl.multiple_of(v0 + i * 8, 8), 8)
            values = [met[m, at_v, :] for m in range(NB)]
            sums = [None] * NB
            roots = None
            for m in range(NB):
                for k in range(m + 1, NB):
                    gap = values[m] - values[k]
                    square = gap * gap + EPS2
                    inverse = lax.rsqrt(square)
                    sign = gap * inverse
                    root = square * inverse
                    roots = root if roots is None else roots + root
                    sums[m] = sign if sums[m] is None else sums[m] + sign
                    sums[k] = -sign if sums[k] is None else sums[k] - sign
            for m in range(NB):
                signs[m, at_v, :] = sums[m]
            spread = roots - (NB * (NB - 1) // 2) * SMOOTHING
            spread = (-COEFF * area_here) * scale_col[at_v, 0:1] * spread
            loss_acc[at_v, :] += spread[:, 0:128] + spread[:, 128:256]

        @pl.loop(1, NB)
        def _(t):
            send_sign(c, lax.rem(member + t, NB)).start()

        keep_sign(c).start()

    def send_part(c, t):
        v0, n = CHUNKS[c]
        j = lax.rem(q + t, 8)
        return pltpu.make_async_remote_copy(
            src_ref=part.at[j, pl.ds(v0, n)],
            dst_ref=part_in.at[t - 1, pl.ds(v0, n)],
            send_sem=rs1_send.at[c, t - 1],
            recv_sem=rs1_recv.at[c],
            device_id=beside(j),
            device_id_type=MESH,
        )

    lane = lax.broadcasted_iota(jnp.int32, (1, 128), 1)
    sub = lax.broadcasted_iota(jnp.int32, (8, 128), 0)

    def extras():
        bias = jnp.sum(bias_acc[...], axis=1, keepdims=True)
        eye = lax.broadcasted_iota(jnp.int32, (VP, 128), 0) == lax.broadcasted_iota(
            jnp.int32, (VP, 128), 1
        )
        extra = jnp.sum(jnp.where(eye, bias, 0.0), axis=0, keepdims=True)
        loss_here = jnp.sum(jnp.sum(loss_acc[...], axis=0, keepdims=True), axis=1, keepdims=True)
        points_here = jnp.float32(0.0)
        for r in range(ROWS):
            points_here += area_ref[space * ROWS + r] * counts_ref[r].astype(F32)
        extra = jnp.where(lane < V, extra, 0.0)
        extra = jnp.where(lane == V, loss_here, extra)
        extra = jnp.where(lane == V + 1, points_here, extra)
        part[0, 96:VP, :] = jnp.where(sub == V - 96, extra, part[0, 96:VP, :])

    def gradient(c):
        v0, n = CHUNKS[c]
        arrived = back.at[:, pl.ds(v0, SENT[c])]
        pltpu.make_async_copy(arrived, arrived, ret_recv.at[c]).wait()
        padded = max(n, 16)
        for b in range(NB):
            point_weight = jnp.where(live(b), area_ref[space * ROWS + b // 2] * COEFF, 0.0)
            factor = point_weight * scale_col[v0 : v0 + n, 0:1]
            value = obs[b, v0 : v0 + n, :] - factor * back[b, v0 : v0 + n, :]
            bias_acc[v0 : v0 + n, :] += value[:, 0:128] + value[:, 128:256]
            if padded > n:
                value = jnp.concatenate([value, jnp.zeros((padded - n, BLOCK), F32)], axis=0)
            grad[v0 : v0 + padded, b * BLOCK : (b + 1) * BLOCK] = value.astype(jnp.bfloat16)
        for j in range(0, 8, 2):
            piece = jnp.dot(
                grad[v0 : v0 + padded, :],
                hbuf[:, j * 128 : (j + 2) * 128],
                preferred_element_type=F32,
            )
            part[j, v0 : v0 + n, :] = piece[0:n, 0:128]
            part[j + 1, v0 : v0 + n, :] = piece[0:n, 128:256]
        if c == NC - 1:
            extras()

        @pl.loop(1, 8)
        def _(t):
            send_part(c, t).start()

    def owner(o):
        return 2 * o + core

    mine = lax.div(rank, 2)
    owns = lax.rem(rank, 2) == core

    def tiles(c):
        v0, n = CHUNKS[c]
        return v0 // 8, (v0 + n) // 8

    def send_plane(o):
        p = owner(o)
        return pltpu.make_async_remote_copy(
            src_ref=plane.at[o],
            dst_ref=plane_in.at[lax.rem(rank - p + 31, 32)],
            send_sem=rs2_send.at[o],
            recv_sem=rs2_recv,
            device_id=at_rank(p),
            device_id_type=MESH,
        )

    def sum_beside(c):
        v0, n = CHUNKS[c]
        arrived = part_in.at[:, pl.ds(v0, n)]
        pltpu.make_async_copy(arrived, arrived, rs1_recv.at[c]).wait()

        @pl.loop(*tiles(c))
        def _(o):
            at_v = pl.ds(pl.multiple_of(o * 8, 8), 8)
            value = part[q, at_v, :]
            for t in range(7):
                value += part_in[t, at_v, :]
            plane[o] = value

            @pl.when(owner(o) != rank)
            def _():
                send_plane(o).start()

    def send_own(t):
        return pltpu.make_async_remote_copy(
            src_ref=own_all.at[mine],
            dst_ref=own_all.at[mine],
            send_sem=ag2_send.at[t - 1],
            recv_sem=ag2_recv.at[mine],
            device_id=at_rank(lax.rem(rank + t, 32)),
            device_id_type=MESH,
        )

    def owns_in(c):
        first, end = tiles(c)
        return jnp.logical_and(owns, jnp.logical_and(mine >= first, mine < end))

    def sum_across(c):
        @pl.when(owns_in(c))
        def _():
            pltpu.make_async_copy(plane_in, plane_in, rs2_recv).wait()
            value = plane[mine]
            for t in range(31):
                value += plane_in[t]
            own_all[mine] = value

            @pl.loop(1, 32)
            def _(t):
                send_own(t).start()

    def send_out(c, t):
        first, end = tiles(c)
        block = pl.ds(first, end - first)
        return pltpu.make_async_remote_copy(
            src_ref=own_all.at[block],
            dst_ref=out_in.at[t, block],
            send_sem=ag1_send.at[c, t - 1],
            recv_sem=ag1_recv.at[c],
            device_id=beside(lax.rem(q + t, 8)),
            device_id_type=MESH,
        )

    def spread_out(c):
        first, end = tiles(c)

        @pl.loop(first, end)
        def _(o):
            @pl.when(owner(o) != rank)
            def _():
                pltpu.make_async_copy(own_all.at[o], own_all.at[o], ag2_recv.at[o]).wait()

        @pl.loop(1, 8)
        def _(t):
            send_out(c, t).start()

        out_in[0, first:end] = own_all[first:end]

    def collect(c):
        first, end = tiles(c)
        arrived = out_in.at[pl.ds(1, 7), pl.ds(first, end - first)]
        pltpu.make_async_copy(arrived, arrived, ag1_recv.at[c]).wait()

        @pl.loop(0, 8)
        def _(t):
            cols = pl.ds(pl.multiple_of(lax.rem(q - t + 8, 8) * 128, 128), 128)
            for o in range(first, end):
                sums_ref[o * 8 : (o + 1) * 8, cols] = out_in[t, o]

    def latent(first, end):
        for b in range(first, end):
            rows = slice(b * BLOCK, (b + 1) * BLOCK)
            value = lax.dot_general(
                grad[0:V, rows], weight[...], (((0,), (0,)), ((), ())), preferred_element_type=F32
            )
            latent_ref[rows, :] = (GRAD_SCALE * value).astype(jnp.bfloat16)

    stages = (pairs, gradient, sum_beside, sum_across, spread_out, collect)
    for step in range(NC + len(stages) - 1):
        for i, stage in enumerate(stages):
            c = step - i
            if 0 <= c < NC:
                stage(c)
                if stage is pairs and c + 2 < NC:
                    send_forecasts(c + 2)
                if c == NC - 1 and 1 <= i <= 4:
                    latent(2 * (i - 1), 2 * i)

    for c in range(NC):

        @pl.loop(1, NB)
        def _(t):
            b = lax.rem(member + t, NB)
            send_forecast(c, b).wait_send()
            send_sign(c, b).wait_send()

        @pl.loop(1, 8)
        def _(t):
            send_part(c, t).wait_send()
            send_out(c, t).wait_send()

    @pl.loop(0, TILES)
    def _(o):
        @pl.when(owner(o) != rank)
        def _():
            send_plane(o).wait_send()

    @pl.when(jnp.logical_and(owns, mine < TILES))
    def _():
        @pl.loop(1, 32)
        def _(t):
            send_own(t).wait_send()


def finish_kernel(factor, latent, sums, latent_hbm, wgrad_hbm, bias_ref, loss_ref, wgrad, sem):
    store_latent = pltpu.make_async_copy(latent, latent_hbm, sem.at[0])
    store_latent.start()
    wgrad[...] = sums[0:V, :] * factor
    store_wgrad = pltpu.make_async_copy(wgrad, wgrad_hbm, sem.at[1])
    store_wgrad.start()
    extra = sums[V : V + 1, 0:128]
    lane = lax.broadcasted_iota(jnp.int32, (1, 128), 1)
    total = jnp.sum(jnp.where(lane == V, extra, 0.0), axis=1, keepdims=True)
    points = jnp.sum(jnp.where(lane == V + 1, extra, 0.0), axis=1, keepdims=True)
    bias_ref[...] = extra[:, 0:V] * factor
    loss_ref[...] = total / (V * (points * (1.0 / NB)))
    store_wgrad.wait()
    store_latent.wait()


def per_device(hidden_state, proj_weight, offset, truth, counts, var_weight, total_rows):
    latitude = (np.arange(total_rows) + 0.5) * (LATITUDE_SPAN / total_rows) * (math.pi / 180.0)
    area = jnp.asarray(np.cos(latitude), dtype=F32)
    vmem = pl.BlockSpec(memory_space=pltpu.VMEM)
    smem = pl.BlockSpec(memory_space=pltpu.SMEM)
    hbm = pl.BlockSpec(memory_space=pltpu.HBM)
    dma = pltpu.SemaphoreType.DMA
    bf16 = jnp.bfloat16
    blocks = pltpu.VMEM((NB, VP, BLOCK), F32)
    latent, sums = pl.pallas_call(
        exchange_kernel,
        out_shape=(
            pltpu.VMEM((POINTS, D), bf16),
            pltpu.VMEM((VP, D), F32),
        ),
        in_specs=[smem, smem, vmem, vmem, hbm, hbm, hbm],
        out_specs=(vmem, vmem),
        scratch_shapes=[
            pltpu.VMEM((V, D), bf16),
            pltpu.VMEM((POINTS, D), bf16),
            pltpu.VMEM((V, ROWS, CAP), F32),
            blocks,
            blocks,
            blocks,
            blocks,
            blocks,
            pltpu.VMEM((GP, POINTS), bf16),
            pltpu.VMEM((VP, 128), F32),
            pltpu.VMEM((VP, 128), F32),
            pltpu.VMEM((VP, 128), F32),
            pltpu.VMEM((VP, 128), F32),
            pltpu.VMEM((8, VP, 128), F32),
            pltpu.VMEM((7, VP, 128), F32),
            pltpu.VMEM((TILES, 8, 128), F32),
            pltpu.VMEM((31, 8, 128), F32),
            pltpu.VMEM((TILES, 8, 128), F32),
            pltpu.VMEM((8, TILES, 8, 128), F32),
            dma((NB,)),
            dma((2,)),
            dma((NC, NB)),
            dma((NC,)),
            dma((NC, NB)),
            dma((NC,)),
            dma((NC, 7)),
            dma((NC,)),
            dma((TILES,)),
            dma,
            dma((31,)),
            dma((TILES,)),
            dma((NC, 7)),
            dma((NC,)),
        ],
        compiler_params=pltpu.CompilerParams(
            collective_id=0, has_side_effects=True, vmem_limit_bytes=59 * 1024 * 1024
        ),
        cost_estimate=pl.CostEstimate(
            flops=4 * V * POINTS * D, bytes_accessed=5_000_000, transcendentals=8_000_000
        ),
    )(
        counts,
        area,
        offset.reshape(1, V),
        var_weight.reshape(1, V),
        proj_weight,
        hidden_state.reshape(POINTS, D),
        truth,
    )
    factor = GRAD_SCALE / math.sqrt(NB * total_rows * CAP)
    latent, wgrad, bias, loss = pl.pallas_call(
        lambda *refs: finish_kernel(factor, *refs),
        out_shape=(
            jax.ShapeDtypeStruct((POINTS, D), bf16),
            jax.ShapeDtypeStruct((V, D), F32),
            jax.ShapeDtypeStruct((1, V), F32),
            jax.ShapeDtypeStruct((1, 1), F32),
        ),
        in_specs=[vmem, vmem],
        out_specs=(hbm, hbm, vmem, vmem),
        scratch_shapes=[pltpu.VMEM((V, D), F32), dma((2,))],
        compiler_params=pltpu.CompilerParams(vmem_limit_bytes=16 * 1024 * 1024),
        cost_estimate=pl.CostEstimate(flops=V * D, bytes_accessed=5_000_000, transcendentals=0),
    )(latent, sums)
    return latent.reshape(hidden_state.shape), wgrad, bias.reshape(V), loss.reshape(())


def solution(mesh):
    total_rows = ROWS * mesh.shape["space"]

    def step(*args):
        return per_device(*args, total_rows)

    return jax.shard_map(
        step,
        mesh=mesh,
        in_specs=(
            P("member", "space", None, None),
            P(),
            P(),
            P(None, "space", None),
            P("space"),
            P(),
        ),
        out_specs=(P("member", "space", None, None), P(), P(), P()),
        check_vma=False,
    )
```

time: 85.6 us -> 83.9 us (0.980)
  Pallas kernels: 84.8 us -> 83.2 us
    pallas_call x1, Pallas kernels: 82.2 us -> 80.5 us  [per_device(): pl.pallas_call(exchange_kernel, out_shape=(pltpu.VMEM((POINTS, D), bf16),...]
where the time goes in v2:
time: 83.9 us; the launch traced here: 83.8 us
  Pallas kernels  83.2 us (99%)
    pallas_call x1, Pallas kernels, per_device(): pl.pallas_call(exchange_kernel, out_shape=(pltpu.VMEM((POINTS, D), bf16),...  80.5 us
    pallas_call x1, Pallas kernels, per_device(): pl.pallas_call(lambda *refs: finish_kernel(factor, *refs), out_shape=(jax...  2.67 us

profile of v2, /device:TPU:1, one launch (start us, length us, event | category | flops | bytes accessed | tf_op | source)
XLA Modules:
  0.0 83.8 jit_solution(11533462236528547277)
XLA Ops:
  0.6 80.5 %shard_map.102 = (bf16[2048,1024]{1,0:T(8,128)(2,1)S(1)}, f32[104,1024]{1,0:T(8,128)S(1)}) custom-call(s32[4]{0:T(128)} %counts_ref.1, f32[128]{0:T(128)} %constant.2.clone.area_ref, f32[1,100]{1,0:T(1,128)} %bitcast.8, f32[1,100]{1,0:T(1,128)} %bitcast.9, bf16[100,1024]{1,0:T(8,128)(2,1)} %weight_hbm.1, bf16[2048,1024]{1,0:T(8,128)(2,1)} %bitcast.6, ...), custom_call_target="tpu_custom_call" | custom-call | flops 838860800 | bytes 5000000 | tf_op jit(solution)/shard_map/pallas_call | solution.py:483
  81.2 2.7 %shard_map.103 = (bf16[2048,1024]{1,0:T(8,128)(2,1)}, f32[100,1024]{1,0:T(8,128)}, f32[1,100]{1,0:T(1,128)}, f32[1,1]{1,0:T(1,128)}) custom-call(bf16[2048,1024]{1,0:T(8,128)(2,1)S(1)} %get-tuple-element.10.refs_0_, f32[104,1024]{1,0:T(8,128)S(1)} %get-tuple-element.11.refs_1_), custom_call_target="tpu_custom_call" | custom-call | flops 102400 | bytes 5000000 | tf_op jit(solution)/shard_map/pallas_call | solution.py:542

commit v3 on v1

v3 whole, which is shorter than its diff:
```python
import math

import numpy as np

import jax
import jax.numpy as jnp
from jax import lax
from jax.experimental import pallas as pl
from jax.experimental.pallas import tpu as pltpu
from jax.sharding import PartitionSpec as P

SMOOTHING = 0.05
FAIRNESS = 0.95
GRAD_SCALE = 16.0
LATITUDE_SPAN = 80.0

V = 100
VP = 104
GP = 112
D = 1024
ROWS = 4
CAP = 512
POINTS = ROWS * CAP
BLOCK = 256
NB = 8
NT = 25
CHUNKS = ((0, 8), (8, 8), (16, 4), (20, 5))
NC = len(CHUNKS)
GROUPS = ((0, 64), (64, 16))
LAST = 80
MESH = pl.DeviceIdType.MESH
F32 = jnp.float32
EPS2 = SMOOTHING * SMOOTHING
COEFF = FAIRNESS / (NB * (NB - 1)) + (1.0 - FAIRNESS) / (NB * NB)


def column(row):
    n = row.shape[1]
    here = lax.broadcasted_iota(jnp.int32, (VP, n), 0) == lax.broadcasted_iota(
        jnp.int32, (VP, n), 1
    )
    return jnp.sum(jnp.where(here, jnp.broadcast_to(row, (VP, n)), 0.0), axis=1, keepdims=True)


def exchange_kernel(
    counts_ref,
    area_ref,
    offset_ref,
    scale_ref,
    weight_hbm,
    hidden_hbm,
    truth_hbm,
    latent_ref,
    sums_ref,
    weight,
    hbuf,
    truth,
    field,
    met,
    signs,
    back,
    obs,
    grad,
    loss_acc,
    bias_acc,
    scale,
    part,
    part_in,
    plane,
    pair,
    y_in,
    z_out,
    z_in,
    own_all,
    out_in,
    last,
    last_in,
    last_mid,
    last_z,
    last_own,
    last_out,
    load_sem,
    side_sem,
    fwd_send,
    fwd_recv,
    ret_send,
    ret_recv,
    part_send,
    part_recv,
    y_send,
    y_recv,
    z_send,
    z_recv,
    row_send,
    row_recv,
    out_send,
    out_recv,
    last_send,
    last_recv,
):
    member = lax.axis_index("member")
    space = lax.axis_index("space")
    y, z_hi = lax.div(member, 2), lax.rem(member, 2)
    z_lo, q = lax.div(space, 8), lax.rem(space, 8)
    x, core = lax.div(q, 2), lax.rem(q, 2)
    z = z_hi * 4 + z_lo
    in_plane = x * 4 + y
    in_stack = z * 2 + core

    def at(xx, yy, zz, cc):
        return (yy * 2 + lax.div(zz, 4), lax.rem(zz, 4) * 8 + xx * 2 + cc)

    def beside(j):
        return at(lax.div(j, 2), y, z, lax.rem(j, 2))

    def plane_device(w):
        return at(lax.div(w, 4), lax.rem(w, 4), z, core)

    def stack_device(u):
        return at(x, y, lax.div(u, 2), lax.rem(u, 2))

    def block_points(b):
        return pl.ds(pl.multiple_of(b * BLOCK, BLOCK), BLOCK)

    def load(t):
        rows = block_points(lax.rem(member + t, NB))
        return pltpu.make_async_copy(hidden_hbm.at[rows], hbuf.at[rows], load_sem.at[t - 1])

    load_weight = pltpu.make_async_copy(weight_hbm, weight, side_sem.at[0])
    load_weight.start()
    for t in range(1, NB + 1):
        load(t).start()
    load_truth = pltpu.make_async_copy(truth_hbm, truth, side_sem.at[1])
    load_truth.start()

    barrier = pltpu.get_barrier_semaphore()

    def greet(device):
        pl.semaphore_signal(barrier, inc=1, device_id=device, device_id_type=MESH)

    @pl.loop(1, 16)
    def _(t):
        greet(plane_device(lax.rem(in_plane + t, 16)))
        greet(stack_device(lax.rem(in_stack + t, 16)))

    @pl.loop(1, 4)
    def _(t):
        greet(at(x, lax.rem(y + t, 4), lax.rem(z + 4, 8), core))
        greet(at(lax.rem(x + t, 4), y, z, 1 - core))

    offsets = column(offset_ref[...])[0:V]
    scales = jnp.broadcast_to(column(scale_ref[...]), (VP, 128))
    for i in range(NT // 2):
        scale[2 * i] = scales[8 * i : 8 * i + 8]
        scale[2 * i + 1] = scales[8 * i : 8 * i + 8]
    scale[NT - 1] = jnp.concatenate([scales[96:V], scales[96:V]], axis=0)
    loss_acc[...] = jnp.zeros_like(loss_acc)
    bias_acc[...] = jnp.zeros_like(bias_acc)

    lane = lax.broadcasted_iota(jnp.int32, (1, 128), 1)
    sub = lax.broadcasted_iota(jnp.int32, (8, 128), 0)

    def live(b, h):
        return lane + (lax.rem(b, 2) * 2 + h) * 128 < counts_ref[lax.div(b, 2)]

    def point_weights(b, factor):
        area = area_ref[space * ROWS + lax.div(b, 2)] * factor
        halves = [jnp.where(live(b, h), area, 0.0) for h in range(2)]
        return halves, jnp.where(sub < 4, halves[0], halves[1])

    def send_forecast(c, b):
        block = pl.ds(*CHUNKS[c])
        return pltpu.make_async_remote_copy(
            src_ref=field.at[b, block],
            dst_ref=met.at[member, block],
            send_sem=fwd_send.at[c, b],
            recv_sem=fwd_recv.at[c],
            device_id=(b, space),
            device_id_type=MESH,
        )

    def keep_forecast(c):
        block = pl.ds(*CHUNKS[c])
        return pltpu.make_async_copy(
            field.at[member, block], met.at[member, block], fwd_recv.at[c]
        )

    for t in range(1, NB + 1):
        load(t).wait()
        if t == 1:
            load_weight.wait()
        b = lax.rem(member + t, NB)
        product = lax.dot_general(
            weight[...],
            hbuf[block_points(b), :],
            (((1,), (1,)), ((), ())),
            preferred_element_type=F32,
        )
        forecast = product + offsets
        halves = [
            jnp.where(live(b, h), forecast[:, h * 128 : (h + 1) * 128], 0.0) for h in range(2)
        ]
        for i in range(NT // 2):
            for h in range(2):
                field[b, 2 * i + h] = halves[h][8 * i : 8 * i + 8]
        field[b, NT - 1] = jnp.concatenate([halves[0][96:V], halves[1][96:V]], axis=0)
        if t == 1:
            pl.semaphore_wait(barrier, 36)
        for c in range(2):
            if t < NB:
                send_forecast(c, b).start()
            else:
                keep_forecast(c).start()
    for c in range(2, NC):

        @pl.loop(1, NB)
        def _(t):
            send_forecast(c, lax.rem(member + t, NB)).start()

        keep_forecast(c).start()

    load_truth.wait()

    def misfit(b, tile, target, weight_here):
        gap = field[b, tile] - target
        square = gap * gap + EPS2
        inverse = lax.rsqrt(square)
        factor = weight_here * scale[tile]
        obs[b, tile] = factor * (gap * inverse)
        return factor * (square * inverse - SMOOTHING)

    def target(b, v, h):
        first = (b % 2) * BLOCK + h * 128
        return truth[v, b // 2, first : first + 128]

    @pl.loop(0, NT // 2)
    def _(i):
        at_v = pl.ds(pl.multiple_of(i * 8, 8), 8)
        total = jnp.zeros((8, 128), F32)
        for b in range(NB):
            halves, _ = point_weights(b, 1.0 / NB)
            for h in range(2):
                total += misfit(b, 2 * i + h, target(b, at_v, h), halves[h])
        loss_acc[...] += total

    total = jnp.zeros((8, 128), F32)
    for b in range(NB):
        _, both = point_weights(b, 1.0 / NB)
        tail = pl.ds(96, 4)
        goal = jnp.concatenate([target(b, tail, 0), target(b, tail, 1)], axis=0)
        total += misfit(b, NT - 1, goal, both)
    loss_acc[...] += total

    area_here = area_ref[space * ROWS + y]

    def send_sign(c, m):
        block = pl.ds(*CHUNKS[c])
        return pltpu.make_async_remote_copy(
            src_ref=signs.at[m, block],
            dst_ref=back.at[member, block],
            send_sem=ret_send.at[c, m],
            recv_sem=ret_recv.at[c],
            device_id=(m, space),
            device_id_type=MESH,
        )

    def keep_sign(c):
        block = pl.ds(*CHUNKS[c])
        return pltpu.make_async_copy(
            signs.at[member, block], back.at[member, block], ret_recv.at[c]
        )

    def arrive(ref, sem):
        pltpu.make_async_copy(ref, ref, sem).wait()

    def meet(block):
        values = [met[m, block] for m in range(NB)]
        sums = [None] * NB
        roots = None
        for m in range(NB):
            for k in range(m + 1, NB):
                gap = values[m] - values[k]
                square = gap * gap + EPS2
                inverse = lax.rsqrt(square)
                sign = gap * inverse
                root = square * inverse
                roots = root if roots is None else roots + root
                sums[m] = sign if sums[m] is None else sums[m] + sign
                sums[k] = -sign if sums[k] is None else sums[k] - sign
        for m in range(NB):
            signs[m, block] = sums[m]
        spread = (roots - (NB * (NB - 1) // 2) * SMOOTHING) * scale[block]
        loss_acc[...] += (-COEFF * area_here) * jnp.sum(spread, axis=0)

    def pairs(c):
        first, n = CHUNKS[c]
        arrive(met.at[:, pl.ds(first, n)], fwd_recv.at[c])

        @pl.loop(0, n // 2)
        def _(i):
            meet(pl.ds(first + 2 * i, 2))

        if n % 2:
            meet(pl.ds(first + n - 1, 1))

        @pl.loop(1, NB)
        def _(t):
            send_sign(c, lax.rem(member + t, NB)).start()

        keep_sign(c).start()

    def gradient(c):
        first, n = CHUNKS[c]
        v0 = 4 * first
        arrive(back.at[:, pl.ds(first, n)], ret_recv.at[c])

        @pl.loop(0, NB)
        def _(b):
            halves, both = point_weights(b, COEFF)

            def value(tile, weight_here):
                result = obs[b, tile] - (weight_here * scale[tile]) * back[b, tile]
                bias_acc[tile] += result
                return result

            pieces = [
                [value(first + 2 * i + h, halves[h]) for i in range(n // 2)] for h in range(2)
            ]
            if n % 2:
                tail = value(NT - 1, both)
                for h in range(2):
                    pieces[h] += [tail[4 * h : 4 * h + 4], jnp.zeros((GP - V, 128), F32)]
            for h in range(2):
                stacked = jnp.concatenate(pieces[h], axis=0)
                points = pl.ds(pl.multiple_of(b * BLOCK + h * 128, 128), 128)
                grad[v0 : v0 + stacked.shape[0], points] = stacked.astype(jnp.bfloat16)

        @pl.loop(0, 4)
        def _(j):
            rows = GP - v0 if n % 2 else 4 * n
            piece = jnp.dot(
                grad[v0 : v0 + rows, :],
                hbuf[:, pl.ds(pl.multiple_of(j * 256, 256), 256)],
                preferred_element_type=F32,
            )
            for k in range(2):
                block = piece[:, k * 128 : (k + 1) * 128]
                if n % 2:
                    for i in range(6):
                        last[4 * j + 2 * k + i // 3, i % 3] = block[4 * i : 4 * i + 4]
                else:
                    part[2 * j + k, v0 : v0 + rows, :] = block

    def extras():
        rows = []
        for i in range(NT // 2):
            rows.append(bias_acc[2 * i] + bias_acc[2 * i + 1])
        tail = bias_acc[NT - 1]
        rows += [tail[0:4] + tail[4:8], jnp.zeros((VP - V, 128), F32)]
        bias = jnp.sum(jnp.concatenate(rows, axis=0), axis=1, keepdims=True)
        eye = lax.broadcasted_iota(jnp.int32, (VP, 128), 0) == lax.broadcasted_iota(
            jnp.int32, (VP, 128), 1
        )
        extra = jnp.sum(jnp.where(eye, bias, 0.0), axis=0, keepdims=True)
        loss_here = jnp.sum(jnp.sum(loss_acc[...], axis=0, keepdims=True), axis=1, keepdims=True)
        points_here = jnp.float32(0.0)
        for r in range(ROWS):
            points_here += area_ref[space * ROWS + r] * counts_ref[r].astype(F32)
        extra = jnp.where(lane == V, loss_here, extra)
        extra = jnp.where(lane == V + 1, points_here, extra)
        last[1, 2, 0:1, :] = extra

    def tiles(g):
        first, n = GROUPS[g]
        return first // 8, (first + n) // 8

    def send_part(g, t):
        rows = pl.ds(*GROUPS[g])
        j = lax.rem(q + t, 8)
        return pltpu.make_async_remote_copy(
            src_ref=part.at[j, rows],
            dst_ref=part_in.at[t - 1, rows],
            send_sem=part_send.at[g, t - 1],
            recv_sem=part_recv.at[g],
            device_id=beside(j),
            device_id_type=MESH,
        )

    def send_plane(g, t):
        yy = lax.rem(y + t, 4)
        return pltpu.make_async_remote_copy(
            src_ref=plane.at[yy] if g == 0 else pair,
            dst_ref=y_in.at[g, y],
            send_sem=y_send.at[g, t - 1],
            recv_sem=y_recv.at[g],
            device_id=at(x, yy, z, core),
            device_id_type=MESH,
        )

    def send_across(g, t):
        return pltpu.make_async_remote_copy(
            src_ref=z_out.at[g],
            dst_ref=z_in.at[g, z],
            send_sem=z_send.at[g, t - 1],
            recv_sem=z_recv.at[g],
            device_id=at(x, y, lax.rem(z + t, 8), core),
            device_id_type=MESH,
        )

    def send_row(t):
        block = own_all.at[pl.ds(2 * y, 2)]
        return pltpu.make_async_remote_copy(
            src_ref=block,
            dst_ref=block,
            send_sem=row_send.at[t - 1],
            recv_sem=row_recv,
            device_id=at(x, lax.rem(y + t, 4), z, core),
            device_id_type=MESH,
        )

    def send_out(g, t):
        first, end = tiles(g)
        block = pl.ds(first, end - first)
        return pltpu.make_async_remote_copy(
            src_ref=own_all.at[block],
            dst_ref=out_in.at[t, block],
            send_sem=out_send.at[g, t - 1],
            recv_sem=out_recv.at[g],
            device_id=beside(lax.rem(q + t, 8)),
            device_id_type=MESH,
        )

    def send_all(send, number):
        @pl.loop(1, number)
        def _(t):
            send(t).start()

    def send_parts(g):
        send_all(lambda t: send_part(g, t), 8)

    def sum_beside(g):
        arrive(part_in.at[:, pl.ds(*GROUPS[g])], part_recv.at[g])

        def column_sum(o):
            at_v = pl.ds(pl.multiple_of(o * 8, 8), 8)
            value = part[q, at_v, :]
            for t in range(7):
                value += part_in[t, at_v, :]
            return value

        if g == 0:

            @pl.loop(0, 4)
            def _(yy):
                for i in range(2):
                    plane[yy, i] = column_sum(2 * yy + i)

            y_in[g, y] = plane[y]
        else:
            for i in range(2):
                pair[i] = column_sum(8 + i)
            y_in[g, y] = pair[...]
        send_all(lambda t: send_plane(g, t), 4)

    def sum_plane(g):
        arrive(y_in.at[g, pl.ds(0, 3)], y_recv.at[g])
        value = y_in[g, 0]
        for yy in range(1, 4):
            value += y_in[g, yy]
        z_out[g] = value
        z_in[g, z] = value
        send_all(lambda t: send_across(g, t), 8)

    def spread_out(g):
        first, end = tiles(g)
        send_all(lambda t: send_out(g, t), 8)
        out_in[0, first:end] = own_all[first:end]

    def sum_across(g):
        arrive(z_in.at[g, pl.ds(0, 7)], z_recv.at[g])
        value = z_in[g, 0]
        for zz in range(1, 8):
            value += z_in[g, zz]
        if g == 0:
            own_all[pl.ds(2 * y, 2)] = value
            send_all(send_row, 4)
        else:
            own_all[8:10] = value
            spread_out(1)

    def collect_rows():
        arrive(own_all.at[pl.ds(0, 6)], row_recv)
        spread_out(0)

    def collect(g):
        first, end = tiles(g)
        arrive(out_in.at[pl.ds(1, 7), pl.ds(first, end - first)], out_recv.at[g])

        @pl.loop(0, 8)
        def _(t):
            cols = pl.ds(pl.multiple_of(lax.rem(q - t + 8, 8) * 128, 128), 128)
            for o in range(first, end):
                sums_ref[o * 8 : (o + 1) * 8, cols] = out_in[t, o]

    def last_copy(phase, t):
        if phase == 1:
            to = lax.rem(in_stack + t, 16)
            src, dst, device = last_mid, last_z.at[in_stack], stack_device(to)
        else:
            to = lax.rem(in_plane + t, 16)
            src = last.at[to] if phase == 0 else last_own
            dst = (last_in if phase == 0 else last_out).at[in_plane]
            device = plane_device(to)
        return pltpu.make_async_remote_copy(
            src_ref=src,
            dst_ref=dst,
            send_sem=last_send.at[phase, t - 1],
            recv_sem=last_recv.at[phase],
            device_id=device,
            device_id_type=MESH,
        )

    def last_start(phase):
        send_all(lambda t: last_copy(phase, t), 16)

    def last_sum(phase, source):
        arrive(source.at[pl.ds(0, 15)], last_recv.at[phase])
        value = source[0]
        for t in range(1, 16):
            value += source[t]
        return value

    def last_scatter():
        last_start(0)
        last_in[in_plane] = last[in_plane]

    def last_across():
        value = last_sum(0, last_in)
        last_mid[...] = value
        last_start(1)
        last_z[in_stack] = value

    def last_gather():
        value = last_sum(1, last_z)
        last_own[...] = value
        last_start(2)
        last_out[in_plane] = value

    def last_collect():
        arrive(last_out.at[pl.ds(0, 15)], last_recv.at[2])

        @pl.loop(0, 8)
        def _(j):
            cols = pl.ds(pl.multiple_of(j * 128, 128), 128)
            for i in range(6):
                rows = slice(LAST + 4 * i, LAST + 4 * i + 4)
                sums_ref[rows, cols] = last_out[2 * j + i // 3, i % 3]

    def latent(first, end):
        @pl.loop(first, end)
        def _(b):
            points = block_points(b)
            value = lax.dot_general(
                grad[0:V, points], weight[...], (((0,), (0,)), ((), ())), preferred_element_type=F32
            )
            latent_ref[points, :] = (GRAD_SCALE * value).astype(jnp.bfloat16)

    for c in range(NC):
        pairs(c)
    gradient(0)
    gradient(1)
    send_parts(0)
    gradient(2)
    send_parts(1)
    sum_beside(0)
    gradient(3)
    extras()
    last_scatter()
    sum_plane(0)
    sum_beside(1)
    latent(0, 2)
    last_across()
    sum_across(0)
    sum_plane(1)
    latent(2, 4)
    last_gather()
    collect_rows()
    sum_across(1)
    latent(4, 8)
    last_collect()
    collect(0)
    collect(1)

    @pl.loop(1, NB)
    def _(t):
        b = lax.rem(member + t, NB)
        for c in range(NC):
            send_forecast(c, b).wait_send()
            send_sign(c, b).wait_send()
        for g in range(len(GROUPS)):
            send_part(g, t).wait_send()
            send_across(g, t).wait_send()
            send_out(g, t).wait_send()

    @pl.loop(1, 4)
    def _(t):
        for g in range(len(GROUPS)):
            send_plane(g, t).wait_send()
        send_row(t).wait_send()

    @pl.loop(1, 16)
    def _(t):
        for phase in range(3):
            last_copy(phase, t).wait_send()


def finish_kernel(factor, latent, sums, latent_hbm, wgrad_hbm, bias_ref, loss_ref, wgrad, sem):
    stores = []
    for b in range(4):
        rows = pl.ds(b * CAP, CAP)
        stores.append(pltpu.make_async_copy(latent.at[rows], latent_hbm.at[rows], sem.at[b]))
        stores[-1].start()
    wgrad[...] = sums[0:V, :] * factor
    stores.append(pltpu.make_async_copy(wgrad, wgrad_hbm, sem.at[4]))
    stores[-1].start()
    extra = sums[V : V + 1, 0:128]
    lane = lax.broadcasted_iota(jnp.int32, (1, 128), 1)
    total = jnp.sum(jnp.where(lane == V, extra, 0.0), axis=1, keepdims=True)
    points = jnp.sum(jnp.where(lane == V + 1, extra, 0.0), axis=1, keepdims=True)
    bias_ref[...] = extra[:, 0:V] * factor
    loss_ref[...] = total / (V * (points * (1.0 / NB)))
    for store in stores:
        store.wait()


def per_device(hidden_state, proj_weight, offset, truth, counts, var_weight, total_rows):
    latitude = (np.arange(total_rows) + 0.5) * (LATITUDE_SPAN / total_rows) * (math.pi / 180.0)
    area = jnp.asarray(np.cos(latitude), dtype=F32)
    vmem = pl.BlockSpec(memory_space=pltpu.VMEM)
    smem = pl.BlockSpec(memory_space=pltpu.SMEM)
    hbm = pl.BlockSpec(memory_space=pltpu.HBM)
    dma = pltpu.SemaphoreType.DMA
    bf16 = jnp.bfloat16
    blocks = pltpu.VMEM((NB, NT, 8, 128), F32)
    half_tiles = (3, 4, 128)
    latent, sums = pl.pallas_call(
        exchange_kernel,
        out_shape=(
            pltpu.VMEM((POINTS, D), bf16),
            pltpu.VMEM((VP, D), F32),
        ),
        in_specs=[smem, smem, vmem, vmem, hbm, hbm, hbm],
        out_specs=(vmem, vmem),
        scratch_shapes=[
            pltpu.VMEM((V, D), bf16),
            pltpu.VMEM((POINTS, D), bf16),
            pltpu.VMEM((V, ROWS, CAP), F32),
            blocks,
            blocks,
            blocks,
            blocks,
            blocks,
            pltpu.VMEM((GP, POINTS), bf16),
            pltpu.VMEM((8, 128), F32),
            pltpu.VMEM((NT, 8, 128), F32),
            pltpu.VMEM((NT, 8, 128), F32),
            pltpu.VMEM((8, LAST, 128), F32),
            pltpu.VMEM((7, LAST, 128), F32),
            pltpu.VMEM((4, 2, 8, 128), F32),
            pltpu.VMEM((2, 8, 128), F32),
            pltpu.VMEM((2, 4, 2, 8, 128), F32),
            pltpu.VMEM((2, 2, 8, 128), F32),
            pltpu.VMEM((2, 8, 2, 8, 128), F32),
            pltpu.VMEM((LAST // 8, 8, 128), F32),
            pltpu.VMEM((8, LAST // 8, 8, 128), F32),
            pltpu.VMEM((16, *half_tiles), F32),
            pltpu.VMEM((16, *half_tiles), F32),
            pltpu.VMEM(half_tiles, F32),
            pltpu.VMEM((16, *half_tiles), F32),
            pltpu.VMEM(half_tiles, F32),
            pltpu.VMEM((16, *half_tiles), F32),
            dma((NB,)),
            dma((2,)),
            dma((NC, NB)),
            dma((NC,)),
            dma((NC, NB)),
            dma((NC,)),
            dma((2, 7)),
            dma((2,)),
            dma((2, 3)),
            dma((2,)),
            dma((2, 7)),
            dma((2,)),
            dma((3,)),
            dma,
            dma((2, 7)),
            dma((2,)),
            dma((3, 15)),
            dma((3,)),
        ],
        compiler_params=pltpu.CompilerParams(
            collective_id=0, has_side_effects=True, vmem_limit_bytes=59 * 1024 * 1024
        ),
        cost_estimate=pl.CostEstimate(
            flops=6 * V * POINTS * D, bytes_accessed=5_000_000, transcendentals=8_000_000
        ),
    )(
        counts,
        area,
        offset.reshape(1, V),
        var_weight.reshape(1, V),
        proj_weight,
        hidden_state.reshape(POINTS, D),
        truth,
    )
    factor = GRAD_SCALE / math.sqrt(NB * total_rows * CAP)
    latent, wgrad, bias, loss = pl.pallas_call(
        lambda *refs: finish_kernel(factor, *refs),
        out_shape=(
            jax.ShapeDtypeStruct((POINTS, D), bf16),
            jax.ShapeDtypeStruct((V, D), F32),
            jax.ShapeDtypeStruct((1, V), F32),
            jax.ShapeDtypeStruct((1, 1), F32),
        ),
        in_specs=[vmem, vmem],
        out_specs=(hbm, hbm, vmem, vmem),
        scratch_shapes=[pltpu.VMEM((V, D), F32), dma((5,))],
        compiler_params=pltpu.CompilerParams(vmem_limit_bytes=16 * 1024 * 1024),
        cost_estimate=pl.CostEstimate(flops=V * D, bytes_accessed=5_000_000, transcendentals=0),
    )(latent, sums)
    return latent.reshape(hidden_state.shape), wgrad, bias.reshape(V), loss.reshape(())


def solution(mesh):
    total_rows = ROWS * mesh.shape["space"]

    def step(*args):
        return per_device(*args, total_rows)

    return jax.shard_map(
        step,
        mesh=mesh,
        in_specs=(
            P("member", "space", None, None),
            P(),
            P(),
            P(None, "space", None),
            P("space"),
            P(),
        ),
        out_specs=(P("member", "space", None, None), P(), P(), P()),
        check_vma=False,
    )
```

time: 85.6 us -> 80.6 us (0.942)
  Pallas kernels: 84.8 us -> 79.9 us
    pallas_call x1, Pallas kernels: 82.2 us -> 77.2 us  [per_device(): pl.pallas_call(exchange_kernel, out_shape=(pltpu.VMEM((POINTS, D), bf16),...]
where the time goes in v3:
time: 80.6 us; the launch traced here: 80.5 us
  Pallas kernels  79.9 us (99%)
    pallas_call x1, Pallas kernels, per_device(): pl.pallas_call(exchange_kernel, out_shape=(pltpu.VMEM((POINTS, D), bf16),...  77.2 us
    pallas_call x1, Pallas kernels, per_device(): pl.pallas_call(lambda *refs: finish_kernel(factor, *refs), out_shape=(jax...  2.7 us

profile of v3, /device:TPU:1, one launch (start us, length us, event | category | flops | bytes accessed | tf_op | source)
XLA Modules:
  0.0 80.5 jit_solution(12625464095466669721)
XLA Ops:
  0.6 77.2 %shard_map.102 = (bf16[2048,1024]{1,0:T(8,128)(2,1)S(1)}, f32[104,1024]{1,0:T(8,128)S(1)}) custom-call(s32[4]{0:T(128)} %counts_ref.1, f32[128]{0:T(128)} %constant.2.clone.area_ref, f32[1,100]{1,0:T(1,128)} %bitcast.8, f32[1,100]{1,0:T(1,128)} %bitcast.9, bf16[100,1024]{1,0:T(8,128)(2,1)} %weight_hbm.1, bf16[2048,1024]{1,0:T(8,128)(2,1)} %bitcast.6, ...), custom_call_target="tpu_custom_call" | custom-call | flops 1258291200 | bytes 5000000 | tf_op jit(solution)/shard_map/pallas_call | solution.py:646
  77.8 2.7 %shard_map.103 = (bf16[2048,1024]{1,0:T(8,128)(2,1)}, f32[100,1024]{1,0:T(8,128)}, f32[1,100]{1,0:T(1,128)}, f32[1,1]{1,0:T(1,128)}) custom-call(bf16[2048,1024]{1,0:T(8,128)(2,1)S(1)} %get-tuple-element.10.refs_0_, f32[104,1024]{1,0:T(8,128)S(1)} %get-tuple-element.11.refs_1_), custom_call_target="tpu_custom_call" | custom-call | flops 102400 | bytes 5000000 | tf_op jit(solution)/shard_map/pallas_call | solution.py:717

commit v4 on v3

--- a/solution.py
+++ b/solution.py
@@ -138,14 +138,12 @@
     def greet(device):
         pl.semaphore_signal(barrier, inc=1, device_id=device, device_id_type=MESH)
 
-    @pl.loop(1, 16)
-    def _(t):
+    for t in range(1, 16):
         greet(plane_device(lax.rem(in_plane + t, 16)))
         greet(stack_device(lax.rem(in_stack + t, 16)))
-
-    @pl.loop(1, 4)
-    def _(t):
-        greet(at(x, lax.rem(y + t, 4), lax.rem(z + 4, 8), core))
+    for t in range(1, 4):
+        greet(at(x, lax.rem(y + t, 4), lax.rem(z + 2, 8), core))
+        greet(at(x, lax.rem(y + t, 4), lax.rem(z + 6, 8), core))
         greet(at(lax.rem(x + t, 4), y, z, 1 - core))
 
     offsets = column(offset_ref[...])[0:V]
@@ -173,16 +171,10 @@
         return pltpu.make_async_remote_copy(
             src_ref=field.at[b, block],
             dst_ref=met.at[member, block],
-            send_sem=fwd_send.at[c, b],
+            send_sem=fwd_send,
             recv_sem=fwd_recv.at[c],
-            device_id=(b, space),
+            device_id=at(x, lax.div(b, 2), lax.rem(z_lo + 2 + 4 * lax.rem(b, 2), 8), core),
             device_id_type=MESH,
-        )
-
-    def keep_forecast(c):
-        block = pl.ds(*CHUNKS[c])
-        return pltpu.make_async_copy(
-            field.at[member, block], met.at[member, block], fwd_recv.at[c]
         )
 
     for t in range(1, NB + 1):
@@ -205,19 +197,12 @@
                 field[b, 2 * i + h] = halves[h][8 * i : 8 * i + 8]
         field[b, NT - 1] = jnp.concatenate([halves[0][96:V], halves[1][96:V]], axis=0)
         if t == 1:
-            pl.semaphore_wait(barrier, 36)
+            pl.semaphore_wait(barrier, 39)
         for c in range(2):
-            if t < NB:
-                send_forecast(c, b).start()
-            else:
-                keep_forecast(c).start()
+            send_forecast(c, b).start()
     for c in range(2, NC):
-
-        @pl.loop(1, NB)
-        def _(t):
+        for t in range(1, NB + 1):
             send_forecast(c, lax.rem(member + t, NB)).start()
-
-        keep_forecast(c).start()
 
     load_truth.wait()
 
@@ -251,23 +236,20 @@
         total += misfit(b, NT - 1, goal, both)
     loss_acc[...] += total
 
-    area_here = area_ref[space * ROWS + y]
+    z_from = lax.rem(z + 2, 4)
+    block_here = y * 2 + lax.div(lax.rem(z - z_from - 2 + 16, 8), 4)
+    space_from = z_from * 8 + q
+    area_here = area_ref[space_from * ROWS + y]
 
     def send_sign(c, m):
         block = pl.ds(*CHUNKS[c])
         return pltpu.make_async_remote_copy(
             src_ref=signs.at[m, block],
-            dst_ref=back.at[member, block],
-            send_sem=ret_send.at[c, m],
+            dst_ref=back.at[block_here, block],
+            send_sem=ret_send,
             recv_sem=ret_recv.at[c],
-            device_id=(m, space),
+            device_id=(m, space_from),
             device_id_type=MESH,
-        )
-
-    def keep_sign(c):
-        block = pl.ds(*CHUNKS[c])
-        return pltpu.make_async_copy(
-            signs.at[member, block], back.at[member, block], ret_recv.at[c]
         )
 
     def arrive(ref, sem):
@@ -303,11 +285,8 @@
         if n % 2:
             meet(pl.ds(first + n - 1, 1))
 
-        @pl.loop(1, NB)
-        def _(t):
+        for t in range(1, NB + 1):
             send_sign(c, lax.rem(member + t, NB)).start()
-
-        keep_sign(c).start()
 
     def gradient(c):
         first, n = CHUNKS[c]
@@ -380,7 +359,7 @@
         return pltpu.make_async_remote_copy(
             src_ref=part.at[j, rows],
             dst_ref=part_in.at[t - 1, rows],
-            send_sem=part_send.at[g, t - 1],
+            send_sem=part_send,
             recv_sem=part_recv.at[g],
             device_id=beside(j),
             device_id_type=MESH,
@@ -391,7 +370,7 @@
         return pltpu.make_async_remote_copy(
             src_ref=plane.at[yy] if g == 0 else pair,
             dst_ref=y_in.at[g, y],
-            send_sem=y_send.at[g, t - 1],
+            send_sem=y_send.at[g],
             recv_sem=y_recv.at[g],
             device_id=at(x, yy, z, core),
             device_id_type=MESH,
@@ -401,7 +380,7 @@
         return pltpu.make_async_remote_copy(
             src_ref=z_out.at[g],
             dst_ref=z_in.at[g, z],
-            send_sem=z_send.at[g, t - 1],
+            send_sem=z_send.at[g],
             recv_sem=z_recv.at[g],
             device_id=at(x, y, lax.rem(z + t, 8), core),
             device_id_type=MESH,
@@ -412,7 +391,7 @@
         return pltpu.make_async_remote_copy(
             src_ref=block,
             dst_ref=block,
-            send_sem=row_send.at[t - 1],
+            send_sem=row_send,
             recv_sem=row_recv,
             device_id=at(x, lax.rem(y + t, 4), z, core),
             device_id_type=MESH,
@@ -424,15 +403,14 @@
         return pltpu.make_async_remote_copy(
             src_ref=own_all.at[block],
             dst_ref=out_in.at[t, block],
-            send_sem=out_send.at[g, t - 1],
+            send_sem=out_send,
             recv_sem=out_recv.at[g],
             device_id=beside(lax.rem(q + t, 8)),
             device_id_type=MESH,
         )
 
     def send_all(send, number):
-        @pl.loop(1, number)
-        def _(t):
+        for t in range(1, number):
             send(t).start()
 
     def send_parts(g):
@@ -514,7 +492,7 @@
         return pltpu.make_async_remote_copy(
             src_ref=src,
             dst_ref=dst,
-            send_sem=last_send.at[phase, t - 1],
+            send_sem=last_send.at[phase],
             recv_sem=last_recv.at[phase],
             device_id=device,
             device_id_type=MESH,
@@ -591,27 +569,17 @@
     collect(0)
     collect(1)
 
-    @pl.loop(1, NB)
-    def _(t):
-        b = lax.rem(member + t, NB)
-        for c in range(NC):
-            send_forecast(c, b).wait_send()
-            send_sign(c, b).wait_send()
-        for g in range(len(GROUPS)):
-            send_part(g, t).wait_send()
-            send_across(g, t).wait_send()
-            send_out(g, t).wait_send()
-
-    @pl.loop(1, 4)
-    def _(t):
-        for g in range(len(GROUPS)):
-            send_plane(g, t).wait_send()
-        send_row(t).wait_send()
-
-    @pl.loop(1, 16)
-    def _(t):
-        for phase in range(3):
-            last_copy(phase, t).wait_send()
+    arrive(field, fwd_send)
+    arrive(signs, ret_send)
+    arrive(part.at[pl.ds(0, 7)], part_send)
+    arrive(plane.at[pl.ds(0, 3)], y_send.at[0])
+    arrive(plane.at[pl.ds(0, 3)], y_send.at[1])
+    for g in range(len(GROUPS)):
+        arrive(z_in.at[g, pl.ds(0, 7)], z_send.at[g])
+    arrive(own_all.at[pl.ds(0, 6)], row_send)
+    arrive(out_in.at[pl.ds(0, 7)], out_send)
+    for phase in range(3):
+        arrive(last.at[pl.ds(0, 15)], last_send.at[phase])
 
 
 def finish_kernel(factor, latent, sums, latent_hbm, wgrad_hbm, bias_ref, loss_ref, wgrad, sem):
@@ -681,21 +649,21 @@
             pltpu.VMEM((16, *half_tiles), F32),
             dma((NB,)),
             dma((2,)),
-            dma((NC, NB)),
+            dma,
             dma((NC,)),
-            dma((NC, NB)),
+            dma,
             dma((NC,)),
-            dma((2, 7)),
+            dma,
             dma((2,)),
-            dma((2, 3)),
             dma((2,)),
-            dma((2, 7)),
+            dma((2,)),
+            dma((2,)),
+            dma((2,)),
+            dma,
+            dma,
+            dma,
             dma((2,)),
             dma((3,)),
-            dma,
-            dma((2, 7)),
-            dma((2,)),
-            dma((3, 15)),
             dma((3,)),
         ],
         compiler_params=pltpu.CompilerParams(

time: 80.6 us -> 76.7 us (0.952)
  Pallas kernels: 79.9 us -> 75.9 us
    pallas_call x1, Pallas kernels: 77.2 us -> 73.2 us  [per_device(): pl.pallas_call(exchange_kernel, out_shape=(pltpu.VMEM((POINTS, D), bf16),...]
where the time goes in v4:
time: 76.7 us; the launch traced here: 76.6 us
  Pallas kernels  75.9 us (99%)
    pallas_call x1, Pallas kernels, per_device(): pl.pallas_call(exchange_kernel, out_shape=(pltpu.VMEM((POINTS, D), bf16),...  73.2 us
    pallas_call x1, Pallas kernels, per_device(): pl.pallas_call(lambda *refs: finish_kernel(factor, *refs), out_shape=(jax...  2.7 us

profile of v4, /device:TPU:1, one launch (start us, length us, event | category | flops | bytes accessed | tf_op | source)
XLA Modules:
  0.0 76.6 jit_solution(2697947307021355302)
XLA Ops:
  0.6 73.2 %shard_map.102 = (bf16[2048,1024]{1,0:T(8,128)(2,1)S(1)}, f32[104,1024]{1,0:T(8,128)S(1)}) custom-call(s32[4]{0:T(128)} %counts_ref.1, f32[128]{0:T(128)} %constant.2.clone.area_ref, f32[1,100]{1,0:T(1,128)} %bitcast.8, f32[1,100]{1,0:T(1,128)} %bitcast.9, bf16[100,1024]{1,0:T(8,128)(2,1)} %weight_hbm.1, bf16[2048,1024]{1,0:T(8,128)(2,1)} %bitcast.6, ...), custom_call_target="tpu_custom_call" | custom-call | flops 1258291200 | bytes 5000000 | tf_op jit(solution)/shard_map/pallas_call | solution.py:614
  73.9 2.7 %shard_map.103 = (bf16[2048,1024]{1,0:T(8,128)(2,1)}, f32[100,1024]{1,0:T(8,128)}, f32[1,100]{1,0:T(1,128)}, f32[1,1]{1,0:T(1,128)}) custom-call(bf16[2048,1024]{1,0:T(8,128)(2,1)S(1)} %get-tuple-element.10.refs_0_, f32[104,1024]{1,0:T(8,128)S(1)} %get-tuple-element.11.refs_1_), custom_call_target="tpu_custom_call" | custom-call | flops 102400 | bytes 5000000 | tf_op jit(solution)/shard_map/pallas_call | solution.py:685

commit v5 on v4

--- a/solution.py
+++ b/solution.py
@@ -204,8 +204,6 @@
         for t in range(1, NB + 1):
             send_forecast(c, lax.rem(member + t, NB)).start()
 
-    load_truth.wait()
-
     def misfit(b, tile, target, weight_here):
         gap = field[b, tile] - target
         square = gap * gap + EPS2
@@ -218,23 +216,26 @@
         first = (b % 2) * BLOCK + h * 128
         return truth[v, b // 2, first : first + 128]
 
-    @pl.loop(0, NT // 2)
-    def _(i):
-        at_v = pl.ds(pl.multiple_of(i * 8, 8), 8)
+    def misfits():
+        load_truth.wait()
+
+        @pl.loop(0, NT // 2)
+        def _(i):
+            at_v = pl.ds(pl.multiple_of(i * 8, 8), 8)
+            total = jnp.zeros((8, 128), F32)
+            for b in range(NB):
+                halves, _ = point_weights(b, 1.0 / NB)
+                for h in range(2):
+                    total += misfit(b, 2 * i + h, target(b, at_v, h), halves[h])
+            loss_acc[...] += total
+
         total = jnp.zeros((8, 128), F32)
         for b in range(NB):
-            halves, _ = point_weights(b, 1.0 / NB)
-            for h in range(2):
-                total += misfit(b, 2 * i + h, target(b, at_v, h), halves[h])
+            _, both = point_weights(b, 1.0 / NB)
+            tail = pl.ds(96, 4)
+            goal = jnp.concatenate([target(b, tail, 0), target(b, tail, 1)], axis=0)
+            total += misfit(b, NT - 1, goal, both)
         loss_acc[...] += total
-
-    total = jnp.zeros((8, 128), F32)
-    for b in range(NB):
-        _, both = point_weights(b, 1.0 / NB)
-        tail = pl.ds(96, 4)
-        goal = jnp.concatenate([target(b, tail, 0), target(b, tail, 1)], axis=0)
-        total += misfit(b, NT - 1, goal, both)
-    loss_acc[...] += total
 
     z_from = lax.rem(z + 2, 4)
     block_here = y * 2 + lax.div(lax.rem(z - z_from - 2 + 16, 8), 4)
@@ -543,8 +544,11 @@
             )
             latent_ref[points, :] = (GRAD_SCALE * value).astype(jnp.bfloat16)
 
-    for c in range(NC):
-        pairs(c)
+    pairs(0)
+    pairs(1)
+    misfits()
+    pairs(2)
+    pairs(3)
     gradient(0)
     gradient(1)
     send_parts(0)

time: 76.7 us -> 76.7 us (level)
  no operation moved by 1% of the time
where the time goes in v5:
time: 76.7 us; the launch traced here: 76.6 us
  Pallas kernels  75.9 us (99%)
    pallas_call x1, Pallas kernels, per_device(): pl.pallas_call(exchange_kernel, out_shape=(pltpu.VMEM((POINTS, D), bf16),...  73.2 us
    pallas_call x1, Pallas kernels, per_device(): pl.pallas_call(lambda *refs: finish_kernel(factor, *refs), out_shape=(jax...  2.7 us

profile of v5, /device:TPU:1, one launch (start us, length us, event | category | flops | bytes accessed | tf_op | source)
XLA Modules:
  0.0 76.6 jit_solution(16572934637453570423)
XLA Ops:
  0.6 73.2 %shard_map.102 = (bf16[2048,1024]{1,0:T(8,128)(2,1)S(1)}, f32[104,1024]{1,0:T(8,128)S(1)}) custom-call(s32[4]{0:T(128)} %counts_ref.1, f32[128]{0:T(128)} %constant.2.clone.area_ref, f32[1,100]{1,0:T(1,128)} %bitcast.8, f32[1,100]{1,0:T(1,128)} %bitcast.9, bf16[100,1024]{1,0:T(8,128)(2,1)} %weight_hbm.1, bf16[2048,1024]{1,0:T(8,128)(2,1)} %bitcast.6, ...), custom_call_target="tpu_custom_call" | custom-call | flops 1258291200 | bytes 5000000 | tf_op jit(solution)/shard_map/pallas_call | solution.py:618
  73.9 2.7 %shard_map.103 = (bf16[2048,1024]{1,0:T(8,128)(2,1)}, f32[100,1024]{1,0:T(8,128)}, f32[1,100]{1,0:T(1,128)}, f32[1,1]{1,0:T(1,128)}) custom-call(bf16[2048,1024]{1,0:T(8,128)(2,1)S(1)} %get-tuple-element.10.refs_0_, f32[104,1024]{1,0:T(8,128)S(1)} %get-tuple-element.11.refs_1_), custom_call_target="tpu_custom_call" | custom-call | flops 102400 | bytes 5000000 | tf_op jit(solution)/shard_map/pallas_call | solution.py:689

commit v6 on v5

--- a/solution.py
+++ b/solution.py
@@ -24,7 +24,7 @@
 BLOCK = 256
 NB = 8
 NT = 25
-CHUNKS = ((0, 8), (8, 8), (16, 4), (20, 5))
+CHUNKS = ((0, 16), (16, 4), (20, 5))
 NC = len(CHUNKS)
 GROUPS = ((0, 64), (64, 16))
 LAST = 80
@@ -198,9 +198,8 @@
         field[b, NT - 1] = jnp.concatenate([halves[0][96:V], halves[1][96:V]], axis=0)
         if t == 1:
             pl.semaphore_wait(barrier, 39)
-        for c in range(2):
-            send_forecast(c, b).start()
-    for c in range(2, NC):
+        send_forecast(0, b).start()
+    for c in range(1, NC):
         for t in range(1, NB + 1):
             send_forecast(c, lax.rem(member + t, NB)).start()
 
@@ -545,17 +544,15 @@
             latent_ref[points, :] = (GRAD_SCALE * value).astype(jnp.bfloat16)
 
     pairs(0)
+    misfits()
     pairs(1)
-    misfits()
     pairs(2)
-    pairs(3)
     gradient(0)
+    send_parts(0)
     gradient(1)
-    send_parts(0)
-    gradient(2)
     send_parts(1)
     sum_beside(0)
-    gradient(3)
+    gradient(2)
     extras()
     last_scatter()
     sum_plane(0)

time: 76.7 us -> 78.8 us (1.027)
  Pallas kernels: 75.9 us -> 78.1 us
    pallas_call x1, Pallas kernels: 73.2 us -> 75.4 us  [per_device(): pl.pallas_call(exchange_kernel, out_shape=(pltpu.VMEM((POINTS, D), bf16),...]
where the time goes in v6:
time: 78.8 us; the launch traced here: 78.7 us
  Pallas kernels  78.1 us (99%)
    pallas_call x1, Pallas kernels, per_device(): pl.pallas_call(exchange_kernel, out_shape=(pltpu.VMEM((POINTS, D), bf16),...  75.4 us
    pallas_call x1, Pallas kernels, per_device(): pl.pallas_call(lambda *refs: finish_kernel(factor, *refs), out_shape=(jax...  2.7 us

profile of v6, /device:TPU:1, one launch (start us, length us, event | category | flops | bytes accessed | tf_op | source)
XLA Modules:
  0.0 78.7 jit_solution(7530705795947212223)
XLA Ops:
  0.6 75.4 %shard_map.102 = (bf16[2048,1024]{1,0:T(8,128)(2,1)S(1)}, f32[104,1024]{1,0:T(8,128)S(1)}) custom-call(s32[4]{0:T(128)} %counts_ref.1, f32[128]{0:T(128)} %constant.2.clone.area_ref, f32[1,100]{1,0:T(1,128)} %bitcast.8, f32[1,100]{1,0:T(1,128)} %bitcast.9, bf16[100,1024]{1,0:T(8,128)(2,1)} %weight_hbm.1, bf16[2048,1024]{1,0:T(8,128)(2,1)} %bitcast.6, ...), custom_call_target="tpu_custom_call" | custom-call | flops 1258291200 | bytes 5000000 | tf_op jit(solution)/shard_map/pallas_call | solution.py:615
  76.0 2.7 %shard_map.103 = (bf16[2048,1024]{1,0:T(8,128)(2,1)}, f32[100,1024]{1,0:T(8,128)}, f32[1,100]{1,0:T(1,128)}, f32[1,1]{1,0:T(1,128)}) custom-call(bf16[2048,1024]{1,0:T(8,128)(2,1)S(1)} %get-tuple-element.10.refs_0_, f32[104,1024]{1,0:T(8,128)S(1)} %get-tuple-element.11.refs_1_), custom_call_target="tpu_custom_call" | custom-call | flops 102400 | bytes 5000000 | tf_op jit(solution)/shard_map/pallas_call | solution.py:686

commit v7 on v5

--- a/solution.py
+++ b/solution.py
@@ -122,8 +122,11 @@
     def block_points(b):
         return pl.ds(pl.multiple_of(b * BLOCK, BLOCK), BLOCK)
 
+    def turn(t):
+        return lax.rem(member + core + t, NB)
+
     def load(t):
-        rows = block_points(lax.rem(member + t, NB))
+        rows = block_points(turn(t))
         return pltpu.make_async_copy(hidden_hbm.at[rows], hbuf.at[rows], load_sem.at[t - 1])
 
     load_weight = pltpu.make_async_copy(weight_hbm, weight, side_sem.at[0])
@@ -181,7 +184,7 @@
         load(t).wait()
         if t == 1:
             load_weight.wait()
-        b = lax.rem(member + t, NB)
+        b = turn(t)
         product = lax.dot_general(
             weight[...],
             hbuf[block_points(b), :],
@@ -202,7 +205,7 @@
             send_forecast(c, b).start()
     for c in range(2, NC):
         for t in range(1, NB + 1):
-            send_forecast(c, lax.rem(member + t, NB)).start()
+            send_forecast(c, turn(t)).start()
 
     def misfit(b, tile, target, weight_here):
         gap = field[b, tile] - target
@@ -287,7 +290,7 @@
             meet(pl.ds(first + n - 1, 1))
 
         for t in range(1, NB + 1):
-            send_sign(c, lax.rem(member + t, NB)).start()
+            send_sign(c, turn(t)).start()
 
     def gradient(c):
         first, n = CHUNKS[c]

time: 76.7 us -> 78.6 us (1.025)
  Pallas kernels: 75.9 us -> 77.8 us
    pallas_call x1, Pallas kernels: 73.2 us -> 75.1 us  [per_device(): pl.pallas_call(exchange_kernel, out_shape=(pltpu.VMEM((POINTS, D), bf16),...]
where the time goes in v7:
time: 78.6 us; the launch traced here: 78.5 us
  Pallas kernels  77.8 us (99%)
    pallas_call x1, Pallas kernels, per_device(): pl.pallas_call(exchange_kernel, out_shape=(pltpu.VMEM((POINTS, D), bf16),...  75.1 us
    pallas_call x1, Pallas kernels, per_device(): pl.pallas_call(lambda *refs: finish_kernel(factor, *refs), out_shape=(jax...  2.7 us

profile of v7, /device:TPU:1, one launch (start us, length us, event | category | flops | bytes accessed | tf_op | source)
XLA Modules:
  0.0 78.5 jit_solution(4093760125227764692)
XLA Ops:
  0.6 75.1 %shard_map.102 = (bf16[2048,1024]{1,0:T(8,128)(2,1)S(1)}, f32[104,1024]{1,0:T(8,128)S(1)}) custom-call(s32[4]{0:T(128)} %counts_ref.1, f32[128]{0:T(128)} %constant.2.clone.area_ref, f32[1,100]{1,0:T(1,128)} %bitcast.8, f32[1,100]{1,0:T(1,128)} %bitcast.9, bf16[100,1024]{1,0:T(8,128)(2,1)} %weight_hbm.1, bf16[2048,1024]{1,0:T(8,128)(2,1)} %bitcast.6, ...), custom_call_target="tpu_custom_call" | custom-call | flops 1258291200 | bytes 5000000 | tf_op jit(solution)/shard_map/pallas_call | solution.py:621
  75.8 2.7 %shard_map.103 = (bf16[2048,1024]{1,0:T(8,128)(2,1)}, f32[100,1024]{1,0:T(8,128)}, f32[1,100]{1,0:T(1,128)}, f32[1,1]{1,0:T(1,128)}) custom-call(bf16[2048,1024]{1,0:T(8,128)(2,1)S(1)} %get-tuple-element.10.refs_0_, f32[104,1024]{1,0:T(8,128)S(1)} %get-tuple-element.11.refs_1_), custom_call_target="tpu_custom_call" | custom-call | flops 102400 | bytes 5000000 | tf_op jit(solution)/shard_map/pallas_call | solution.py:692

commit v8 on v5

--- a/solution.py
+++ b/solution.py
@@ -183,12 +183,12 @@
             load_weight.wait()
         b = lax.rem(member + t, NB)
         product = lax.dot_general(
+            hbuf[block_points(b), :],
             weight[...],
-            hbuf[block_points(b), :],
             (((1,), (1,)), ((), ())),
             preferred_element_type=F32,
         )
-        forecast = product + offsets
+        forecast = product.T + offsets
         halves = [
             jnp.where(live(b, h), forecast[:, h * 128 : (h + 1) * 128], 0.0) for h in range(2)
         ]

time: 76.7 us -> 76.7 us (level)
  no operation moved by 1% of the time
where the time goes in v8:
time: 76.7 us; the launch traced here: 76.6 us
  Pallas kernels  76 us (99%)
    pallas_call x1, Pallas kernels, per_device(): pl.pallas_call(exchange_kernel, out_shape=(pltpu.VMEM((POINTS, D), bf16),...  73.3 us
    pallas_call x1, Pallas kernels, per_device(): pl.pallas_call(lambda *refs: finish_kernel(factor, *refs), out_shape=(jax...  2.7 us

profile of v8, /device:TPU:1, one launch (start us, length us, event | category | flops | bytes accessed | tf_op | source)
XLA Modules:
  0.0 76.6 jit_solution(16384231637027408608)
XLA Ops:
  0.6 73.3 %shard_map.102 = (bf16[2048,1024]{1,0:T(8,128)(2,1)S(1)}, f32[104,1024]{1,0:T(8,128)S(1)}) custom-call(s32[4]{0:T(128)} %counts_ref.1, f32[128]{0:T(128)} %constant.2.clone.area_ref, f32[1,100]{1,0:T(1,128)} %bitcast.8, f32[1,100]{1,0:T(1,128)} %bitcast.9, bf16[100,1024]{1,0:T(8,128)(2,1)} %weight_hbm.1, bf16[2048,1024]{1,0:T(8,128)(2,1)} %bitcast.6, ...), custom_call_target="tpu_custom_call" | custom-call | flops 1258291200 | bytes 5000000 | tf_op jit(solution)/shard_map/pallas_call | solution.py:618
  73.9 2.7 %shard_map.103 = (bf16[2048,1024]{1,0:T(8,128)(2,1)}, f32[100,1024]{1,0:T(8,128)}, f32[1,100]{1,0:T(1,128)}, f32[1,1]{1,0:T(1,128)}) custom-call(bf16[2048,1024]{1,0:T(8,128)(2,1)S(1)} %get-tuple-element.10.refs_0_, f32[104,1024]{1,0:T(8,128)S(1)} %get-tuple-element.11.refs_1_), custom_call_target="tpu_custom_call" | custom-call | flops 102400 | bytes 5000000 | tf_op jit(solution)/shard_map/pallas_call | solution.py:689

commit v9 on v5

--- a/solution.py
+++ b/solution.py
@@ -104,8 +104,7 @@
     z_lo, q = lax.div(space, 8), lax.rem(space, 8)
     x, core = lax.div(q, 2), lax.rem(q, 2)
     z = z_hi * 4 + z_lo
-    in_plane = x * 4 + y
-    in_stack = z * 2 + core
+    in_plane = (x * 4 + y) * 2 + core
 
     def at(xx, yy, zz, cc):
         return (yy * 2 + lax.div(zz, 4), lax.rem(zz, 4) * 8 + xx * 2 + cc)
@@ -114,10 +113,10 @@
         return at(lax.div(j, 2), y, z, lax.rem(j, 2))
 
     def plane_device(w):
-        return at(lax.div(w, 4), lax.rem(w, 4), z, core)
-
-    def stack_device(u):
-        return at(x, y, lax.div(u, 2), lax.rem(u, 2))
+        return at(lax.div(w, 8), lax.rem(lax.div(w, 2), 4), z, lax.rem(w, 2))
+
+    def stack_device(zz):
+        return at(x, y, zz, core)
 
     def block_points(b):
         return pl.ds(pl.multiple_of(b * BLOCK, BLOCK), BLOCK)
@@ -138,13 +137,13 @@
     def greet(device):
         pl.semaphore_signal(barrier, inc=1, device_id=device, device_id_type=MESH)
 
-    for t in range(1, 16):
-        greet(plane_device(lax.rem(in_plane + t, 16)))
-        greet(stack_device(lax.rem(in_stack + t, 16)))
+    for t in range(1, 32):
+        greet(plane_device(lax.rem(in_plane + t, 32)))
+    for t in range(1, 8):
+        greet(stack_device(lax.rem(z + t, 8)))
     for t in range(1, 4):
         greet(at(x, lax.rem(y + t, 4), lax.rem(z + 2, 8), core))
         greet(at(x, lax.rem(y + t, 4), lax.rem(z + 6, 8), core))
-        greet(at(lax.rem(x + t, 4), y, z, 1 - core))
 
     offsets = column(offset_ref[...])[0:V]
     scales = jnp.broadcast_to(column(scale_ref[...]), (VP, 128))
@@ -197,7 +196,7 @@
                 field[b, 2 * i + h] = halves[h][8 * i : 8 * i + 8]
         field[b, NT - 1] = jnp.concatenate([halves[0][96:V], halves[1][96:V]], axis=0)
         if t == 1:
-            pl.semaphore_wait(barrier, 39)
+            pl.semaphore_wait(barrier, 44)
         for c in range(2):
             send_forecast(c, b).start()
     for c in range(2, NC):
@@ -289,6 +288,11 @@
         for t in range(1, NB + 1):
             send_sign(c, lax.rem(member + t, NB)).start()
 
+    def weight_sum(v0, rows, first):
+        return jnp.dot(
+            grad[v0 : v0 + rows, :], hbuf[:, pl.ds(first, 256)], preferred_element_type=F32
+        )
+
     def gradient(c):
         first, n = CHUNKS[c]
         v0 = 4 * first
@@ -315,21 +319,14 @@
                 points = pl.ds(pl.multiple_of(b * BLOCK + h * 128, 128), 128)
                 grad[v0 : v0 + stacked.shape[0], points] = stacked.astype(jnp.bfloat16)
 
+        if n % 2:
+            return
+
         @pl.loop(0, 4)
         def _(j):
-            rows = GP - v0 if n % 2 else 4 * n
-            piece = jnp.dot(
-                grad[v0 : v0 + rows, :],
-                hbuf[:, pl.ds(pl.multiple_of(j * 256, 256), 256)],
-                preferred_element_type=F32,
-            )
+            piece = weight_sum(v0, 4 * n, pl.multiple_of(j * 256, 256))
             for k in range(2):
-                block = piece[:, k * 128 : (k + 1) * 128]
-                if n % 2:
-                    for i in range(6):
-                        last[4 * j + 2 * k + i // 3, i % 3] = block[4 * i : 4 * i + 4]
-                else:
-                    part[2 * j + k, v0 : v0 + rows, :] = block
+                part[2 * j + k, v0 : v0 + 4 * n, :] = piece[:, k * 128 : (k + 1) * 128]
 
     def extras():
         rows = []
@@ -348,7 +345,7 @@
             points_here += area_ref[space * ROWS + r] * counts_ref[r].astype(F32)
         extra = jnp.where(lane == V, loss_here, extra)
         extra = jnp.where(lane == V + 1, points_here, extra)
-        last[1, 2, 0:1, :] = extra
+        return extra
 
     def tiles(g):
         first, n = GROUPS[g]
@@ -481,12 +478,10 @@
             for o in range(first, end):
                 sums_ref[o * 8 : (o + 1) * 8, cols] = out_in[t, o]
 
-    def last_copy(phase, t):
+    def last_copy(phase, to):
         if phase == 1:
-            to = lax.rem(in_stack + t, 16)
-            src, dst, device = last_mid, last_z.at[in_stack], stack_device(to)
+            src, dst, device = last_mid, last_z.at[z], stack_device(to)
         else:
-            to = lax.rem(in_plane + t, 16)
             src = last.at[to] if phase == 0 else last_own
             dst = (last_in if phase == 0 else last_out).at[in_plane]
             device = plane_device(to)
@@ -499,41 +494,54 @@
             device_id_type=MESH,
         )
 
-    def last_start(phase):
-        send_all(lambda t: last_copy(phase, t), 16)
-
-    def last_sum(phase, source):
-        arrive(source.at[pl.ds(0, 15)], last_recv.at[phase])
+    def last_sum(phase, source, number):
+        arrive(source.at[pl.ds(0, number - 1)], last_recv.at[phase])
         value = source[0]
-        for t in range(1, 16):
+        for t in range(1, number):
             value += source[t]
         return value
 
     def last_scatter():
-        last_start(0)
+        extra = extras()
+        for j in (1, 2, 3, 0):
+            piece = weight_sum(LAST, GP - LAST, j * 256)
+            for k in range(2):
+                block = piece[:, k * 128 : (k + 1) * 128]
+                for i in range(12):
+                    last[8 * j + 4 * k + i // 3, i % 3] = block[2 * i : 2 * i + 2]
+            if j == 0:
+                last[3, 1, 0:1, :] = extra
+            for p in range(8 * j, 8 * j + 8):
+
+                @pl.when(in_plane != p)
+                def _():
+                    last_copy(0, p).start()
+
         last_in[in_plane] = last[in_plane]
 
     def last_across():
-        value = last_sum(0, last_in)
+        value = last_sum(0, last_in, 32)
         last_mid[...] = value
-        last_start(1)
-        last_z[in_stack] = value
+        for t in range(1, 8):
+            last_copy(1, lax.rem(z + t, 8)).start()
+        last_z[z] = value
 
     def last_gather():
-        value = last_sum(1, last_z)
+        value = last_sum(1, last_z, 8)
         last_own[...] = value
-        last_start(2)
+        for t in range(1, 32):
+            last_copy(2, lax.rem(in_plane + t, 32)).start()
         last_out[in_plane] = value
 
     def last_collect():
-        arrive(last_out.at[pl.ds(0, 15)], last_recv.at[2])
+        arrive(last_out.at[pl.ds(0, 31)], last_recv.at[2])
 
         @pl.loop(0, 8)
         def _(j):
             cols = pl.ds(pl.multiple_of(j * 128, 128), 128)
-            for i in range(6):
-                rows = slice(LAST + 4 * i, LAST + 4 * i + 4)
-                sums_ref[rows, cols] = last_out[2 * j + i // 3, i % 3]
+            for i in range(12):
+                rows = slice(LAST + 2 * i, LAST + 2 * i + 2)
+                sums_ref[rows, cols] = last_out[4 * j + i // 3, i % 3]
 
     def latent(first, end):
         @pl.loop(first, end)
@@ -556,7 +564,6 @@
     send_parts(1)
     sum_beside(0)
     gradient(3)
-    extras()
     last_scatter()
     sum_plane(0)
     sum_beside(1)
@@ -582,8 +589,8 @@
         arrive(z_in.at[g, pl.ds(0, 7)], z_send.at[g])
     arrive(own_all.at[pl.ds(0, 6)], row_send)
     arrive(out_in.at[pl.ds(0, 7)], out_send)
-    for phase in range(3):
-        arrive(last.at[pl.ds(0, 15)], last_send.at[phase])
+    for phase, number in enumerate((31, 7, 31)):
+        arrive(last.at[pl.ds(0, number)], last_send.at[phase])
 
 
 def finish_kernel(factor, latent, sums, latent_hbm, wgrad_hbm, bias_ref, loss_ref, wgrad, sem):
@@ -614,7 +621,7 @@
     dma = pltpu.SemaphoreType.DMA
     bf16 = jnp.bfloat16
     blocks = pltpu.VMEM((NB, NT, 8, 128), F32)
-    half_tiles = (3, 4, 128)
+    few_rows = (3, 2, 128)
     latent, sums = pl.pallas_call(
         exchange_kernel,
         out_shape=(
@@ -645,12 +652,12 @@
             pltpu.VMEM((2, 8, 2, 8, 128), F32),
             pltpu.VMEM((LAST // 8, 8, 128), F32),
             pltpu.VMEM((8, LAST // 8, 8, 128), F32),
-            pltpu.VMEM((16, *half_tiles), F32),
-            pltpu.VMEM((16, *half_tiles), F32),
-            pltpu.VMEM(half_tiles, F32),
-            pltpu.VMEM((16, *half_tiles), F32),
-            pltpu.VMEM(half_tiles, F32),
-            pltpu.VMEM((16, *half_tiles), F32),
+            pltpu.VMEM((32, *few_rows), F32),
+            pltpu.VMEM((32, *few_rows), F32),
+            pltpu.VMEM(few_rows, F32),
+            pltpu.VMEM((8, *few_rows), F32),
+            pltpu.VMEM(few_rows, F32),
+            pltpu.VMEM((32, *few_rows), F32),
             dma((NB,)),
             dma((2,)),
             dma,

time: 76.7 us -> 75 us (0.978)
  Pallas kernels: 75.9 us -> 74.3 us
    pallas_call x1, Pallas kernels: 73.2 us -> 71.6 us  [per_device(): pl.pallas_call(exchange_kernel, out_shape=(pltpu.VMEM((POINTS, D), bf16),...]
where the time goes in v9:
time: 75 us
  Pallas kernels  74.3 us (99%)
    pallas_call x1, Pallas kernels, per_device(): pl.pallas_call(exchange_kernel, out_shape=(pltpu.VMEM((POINTS, D), bf16),...  71.6 us
    pallas_call x1, Pallas kernels, per_device(): pl.pallas_call(lambda *refs: finish_kernel(factor, *refs), out_shape=(jax...  2.7 us

profile of v9, /device:TPU:1, one launch (start us, length us, event | category | flops | bytes accessed | tf_op | source)
XLA Modules:
  0.0 75.0 jit_solution(9828102193087710857)
XLA Ops:
  0.6 71.6 %shard_map.102 = (bf16[2048,1024]{1,0:T(8,128)(2,1)S(1)}, f32[104,1024]{1,0:T(8,128)S(1)}) custom-call(s32[4]{0:T(128)} %counts_ref.1, f32[128]{0:T(128)} %constant.2.clone.area_ref, f32[1,100]{1,0:T(1,128)} %bitcast.8, f32[1,100]{1,0:T(1,128)} %bitcast.9, bf16[100,1024]{1,0:T(8,128)(2,1)} %weight_hbm.1, bf16[2048,1024]{1,0:T(8,128)(2,1)} %bitcast.6, ...), custom_call_target="tpu_custom_call" | custom-call | flops 1258291200 | bytes 5000000 | tf_op jit(solution)/shard_map/pallas_call | solution.py:625
  72.3 2.7 %shard_map.103 = (bf16[2048,1024]{1,0:T(8,128)(2,1)}, f32[100,1024]{1,0:T(8,128)}, f32[1,100]{1,0:T(1,128)}, f32[1,1]{1,0:T(1,128)}) custom-call(bf16[2048,1024]{1,0:T(8,128)(2,1)S(1)} %get-tuple-element.10.refs_0_, f32[104,1024]{1,0:T(8,128)S(1)} %get-tuple-element.11.refs_1_), custom_call_target="tpu_custom_call" | custom-call | flops 102400 | bytes 5000000 | tf_op jit(solution)/shard_map/pallas_call | solution.py:696

commit v10 on v9

--- a/solution.py
+++ b/solution.py
@@ -564,21 +564,21 @@
     send_parts(1)
     sum_beside(0)
     gradient(3)
-    last_scatter()
     sum_plane(0)
     sum_beside(1)
+    last_scatter()
+    sum_across(0)
+    sum_plane(1)
     latent(0, 2)
     last_across()
-    sum_across(0)
-    sum_plane(1)
+    collect_rows()
+    sum_across(1)
     latent(2, 4)
     last_gather()
-    collect_rows()
-    sum_across(1)
     latent(4, 8)
-    last_collect()
     collect(0)
     collect(1)
+    last_collect()
 
     arrive(field, fwd_send)
     arrive(signs, ret_send)

time: 75 us -> 76.9 us (1.025)
  Pallas kernels: 74.3 us -> 76.1 us
    pallas_call x1, Pallas kernels: 71.6 us -> 73.4 us  [per_device(): pl.pallas_call(exchange_kernel, out_shape=(pltpu.VMEM((POINTS, D), bf16),...]
where the time goes in v10:
time: 76.9 us; the launch traced here: 76.8 us
  Pallas kernels  76.1 us (99%)
    pallas_call x1, Pallas kernels, per_device(): pl.pallas_call(exchange_kernel, out_shape=(pltpu.VMEM((POINTS, D), bf16),...  73.4 us
    pallas_call x1, Pallas kernels, per_device(): pl.pallas_call(lambda *refs: finish_kernel(factor, *refs), out_shape=(jax...  2.7 us

profile of v10, /device:TPU:1, one launch (start us, length us, event | category | flops | bytes accessed | tf_op | source)
XLA Modules:
  0.0 76.8 jit_solution(1653807548689306772)
XLA Ops:
  0.6 73.4 %shard_map.102 = (bf16[2048,1024]{1,0:T(8,128)(2,1)S(1)}, f32[104,1024]{1,0:T(8,128)S(1)}) custom-call(s32[4]{0:T(128)} %counts_ref.1, f32[128]{0:T(128)} %constant.2.clone.area_ref, f32[1,100]{1,0:T(1,128)} %bitcast.8, f32[1,100]{1,0:T(1,128)} %bitcast.9, bf16[100,1024]{1,0:T(8,128)(2,1)} %weight_hbm.1, bf16[2048,1024]{1,0:T(8,128)(2,1)} %bitcast.6, ...), custom_call_target="tpu_custom_call" | custom-call | flops 1258291200 | bytes 5000000 | tf_op jit(solution)/shard_map/pallas_call | solution.py:625
  74.1 2.7 %shard_map.103 = (bf16[2048,1024]{1,0:T(8,128)(2,1)}, f32[100,1024]{1,0:T(8,128)}, f32[1,100]{1,0:T(1,128)}, f32[1,1]{1,0:T(1,128)}) custom-call(bf16[2048,1024]{1,0:T(8,128)(2,1)S(1)} %get-tuple-element.10.refs_0_, f32[104,1024]{1,0:T(8,128)S(1)} %get-tuple-element.11.refs_1_), custom_call_target="tpu_custom_call" | custom-call | flops 102400 | bytes 5000000 | tf_op jit(solution)/shard_map/pallas_call | solution.py:696

commit v11 on v9

--- a/solution.py
+++ b/solution.py
@@ -562,8 +562,8 @@
     send_parts(0)
     gradient(2)
     send_parts(1)
+    gradient(3)
     sum_beside(0)
-    gradient(3)
     last_scatter()
     sum_plane(0)
     sum_beside(1)

time: 75 us -> 74.9 us (level)
  no operation moved by 1% of the time
where the time goes in v11:
time: 74.9 us; the launch traced here: 74.8 us
  Pallas kernels  74.2 us (99%)
    pallas_call x1, Pallas kernels, per_device(): pl.pallas_call(exchange_kernel, out_shape=(pltpu.VMEM((POINTS, D), bf16),...  71.5 us
    pallas_call x1, Pallas kernels, per_device(): pl.pallas_call(lambda *refs: finish_kernel(factor, *refs), out_shape=(jax...  2.7 us

profile of v11, /device:TPU:1, one launch (start us, length us, event | category | flops | bytes accessed | tf_op | source)
XLA Modules:
  0.0 74.8 jit_solution(1087959287280104775)
XLA Ops:
  0.6 71.5 %shard_map.102 = (bf16[2048,1024]{1,0:T(8,128)(2,1)S(1)}, f32[104,1024]{1,0:T(8,128)S(1)}) custom-call(s32[4]{0:T(128)} %counts_ref.1, f32[128]{0:T(128)} %constant.2.clone.area_ref, f32[1,100]{1,0:T(1,128)} %bitcast.8, f32[1,100]{1,0:T(1,128)} %bitcast.9, bf16[100,1024]{1,0:T(8,128)(2,1)} %weight_hbm.1, bf16[2048,1024]{1,0:T(8,128)(2,1)} %bitcast.6, ...), custom_call_target="tpu_custom_call" | custom-call | flops 1258291200 | bytes 5000000 | tf_op jit(solution)/shard_map/pallas_call | solution.py:625
  72.1 2.7 %shard_map.103 = (bf16[2048,1024]{1,0:T(8,128)(2,1)}, f32[100,1024]{1,0:T(8,128)}, f32[1,100]{1,0:T(1,128)}, f32[1,1]{1,0:T(1,128)}) custom-call(bf16[2048,1024]{1,0:T(8,128)(2,1)S(1)} %get-tuple-element.10.refs_0_, f32[104,1024]{1,0:T(8,128)S(1)} %get-tuple-element.11.refs_1_), custom_call_target="tpu_custom_call" | custom-call | flops 102400 | bytes 5000000 | tf_op jit(solution)/shard_map/pallas_call | solution.py:696
